TPU v7x, 128 devices: a whole 4x4x4 slice. The times are simulated.
128 devices in a mesh: loader: 8 (over z, core), enc: 16 (over x, y).
Axes of the slice: x: 4, y: 4, z: 4, core: 2. Of those that a mesh axis runs over, the one named last changes fastest.
Arguments:
- tiles: bfloat16 [802816, 512], P(('loader', 'enc')), may hold values from -6 to 6
- tile_encoder: int32 [4096], P(('loader', 'enc')), may hold values from -1 to 15, as said below
- tile_slot: int32 [4096], P(('loader', 'enc')), may hold values from -1 to 15, as said below
- slide_counts: int32 [128, 8], P(('loader', 'enc')), may hold values from 0 to 30, as said below
- slide_owner: int32 [1024, 1], P(('loader', 'enc')), may hold values from 0 to 7; in each aligned block of 8 rows (0 to 7, 8 to 15, ...) at most 4 rows name the same one
- w_reduce: bfloat16 [512, 256], replicated, may hold values from -0.25 to 0.25
- b_reduce: float32 [256], replicated, may hold values from -3 to 3
- w_spatial: bfloat16 [2304, 256], replicated, may hold values from -0.125 to 0.125
- b_spatial: float32 [256], replicated, may hold values from -3 to 3
- w_expand: bfloat16 [256, 1024], replicated, may hold values from -0.375 to 0.375
- w_short: bfloat16 [512, 1024], replicated, may hold values from -0.25 to 0.25
- b_join: float32 [1024], replicated, may hold values from -3 to 3
- w_reduce2: bfloat16 [1024, 256], replicated, may hold values from -0.1875 to 0.1875
- b_reduce2: float32 [256], replicated, may hold values from -3 to 3
- w_spatial2: bfloat16 [2304, 256], replicated, may hold values from -0.125 to 0.125
- b_spatial2: float32 [256], replicated, may hold values from -3 to 3
- w_expand2: bfloat16 [256, 1024], replicated, may hold values from -0.375 to 0.375
- b_expand2: float32 [1024], replicated, may hold values from -3 to 3
Outputs:
- slide_features: bfloat16 [4096, 1024], P(('loader', 'enc'))
Inputs may be any that keep to these rules, and one draw needn't show every extreme that they name: `tile_encoder`: on each device the tissue tiles are the first tile places, as many as its slides' counts add up to, and only they have an encoder. A device holds at most 30 tissue tiles, and some device holds that many. The encoder lies in the same loader row. Every encoder device gets exactly 16 tissue tiles from the devices of its loader row, and at most 2 from one device; some device sends 2 to one encoder. `tile_slot`: -1 exactly where tile_encoder is -1; the tissue tiles sent to one encoder hold the places 0 to 15 once each. `slide_counts`: A device's counts add up to its number of tissue tiles; slides may hold no tissue tile; some slide holds 30. `slide_owner`: the owner is a loader index in the same enc column. Of the 8 slides of one device at most 4 go to one owner.
All inputs are finite; a program needn't handle non-finite values.
Results may differ from a plain program's by a relative error of at most 0.0034.
Values may be sent and summed in bfloat16 or wider, within the bound.
A program may use at most 128 MiB of HBM per device.

v0:
```python
import math

import jax
import jax.numpy as jnp
from jax import lax
from jax.sharding import PartitionSpec as P

GRID = 14


def spatial_conv(flat_rows, tile_count, weight, bias_row):
    channels = flat_rows.shape[1]
    out_width = weight.shape[1]
    cells = GRID * GRID
    tap_weights = (
        weight.reshape(9, channels, out_width).transpose(1, 0, 2).reshape(channels, 9 * out_width)
    )
    tap_terms = jnp.dot(flat_rows, tap_weights, preferred_element_type=jnp.float32).reshape(
        tile_count, cells, 9 * out_width
    )
    margin = GRID + 1
    padded = jnp.pad(tap_terms, ((0, 0), (margin, margin), (0, 0)))
    column_of = jnp.arange(cells, dtype=jnp.int32) % GRID
    summed = jnp.zeros((tile_count, cells, out_width), jnp.float32) + bias_row
    for tap_index in range(9):
        row_shift = tap_index // 3 - 1
        col_shift = tap_index % 3 - 1
        offset = row_shift * GRID + col_shift
        piece = padded[
            :,
            margin + offset : margin + offset + cells,
            tap_index * out_width : (tap_index + 1) * out_width,
        ]
        valid = (column_of + col_shift >= 0) & (column_of + col_shift < GRID)
        summed = summed + jnp.where(valid[None, :, None], piece, 0.0)
    return jax.nn.relu(summed).astype(jnp.bfloat16).reshape(tile_count * cells, out_width)


def encode(
    pixels,
    tile_count,
    w_reduce,
    b_reduce,
    w_spatial,
    b_spatial,
    w_expand,
    w_short,
    b_join,
    w_reduce2,
    b_reduce2,
    w_spatial2,
    b_spatial2,
    w_expand2,
    b_expand2,
):
    reduced = jax.nn.relu(
        jnp.dot(pixels, w_reduce, preferred_element_type=jnp.float32) + b_reduce
    ).astype(jnp.bfloat16)
    spatial = spatial_conv(reduced, tile_count, w_spatial, b_spatial)
    joined = jax.nn.relu(
        jnp.dot(spatial, w_expand, preferred_element_type=jnp.float32)
        + jnp.dot(pixels, w_short, preferred_element_type=jnp.float32)
        + b_join
    ).astype(jnp.bfloat16)
    narrowed = jax.nn.relu(
        jnp.dot(joined, w_reduce2, preferred_element_type=jnp.float32) + b_reduce2
    ).astype(jnp.bfloat16)
    spread = spatial_conv(narrowed, tile_count, w_spatial2, b_spatial2)
    block_out = jax.nn.relu(
        jnp.dot(spread, w_expand2, preferred_element_type=jnp.float32)
        + b_expand2
        + joined.astype(jnp.float32)
    )
    return jnp.mean(block_out.reshape(tile_count, GRID * GRID, -1), axis=1).astype(jnp.bfloat16)


def encode_all(rows, total, weights):
    group_size = math.gcd(total, 8)
    grouped = rows.reshape(total // group_size, group_size * GRID * GRID, rows.shape[1])
    pooled = lax.map(lambda block: encode(block, group_size, *weights), grouped)
    return pooled.reshape(total, -1)


def tile_rows_of(places):
    cells = GRID * GRID
    return (places[:, None] * cells + jnp.arange(cells, dtype=jnp.int32)[None, :]).reshape(-1)


def body(
    tiles,
    tile_encoder,
    tile_slot,
    slide_counts,
    slide_owner,
    w_reduce,
    b_reduce,
    w_spatial,
    b_spatial,
    w_expand,
    w_short,
    b_join,
    w_reduce2,
    b_reduce2,
    w_spatial2,
    b_spatial2,
    w_expand2,
    b_expand2,
):
    weights = (
        w_reduce,
        b_reduce,
        w_spatial,
        b_spatial,
        w_expand,
        w_short,
        b_join,
        w_reduce2,
        b_reduce2,
        w_spatial2,
        b_spatial2,
        w_expand2,
        b_expand2,
    )
    cells = GRID * GRID
    channels = tiles.shape[1]
    tile_total = tile_encoder.shape[0]
    encoders = lax.axis_size("enc")
    loaders = lax.axis_size("loader")
    work_tiles = tile_total // 2
    send_cap = 2 * max(1, (2 * work_tiles + 2 * encoders - 7) // (2 * encoders - 2))
    tissue = tile_encoder >= 0
    positions = jnp.arange(tile_total, dtype=jnp.int32)
    earlier = (tile_encoder[None, :] == tile_encoder[:, None]) & (
        positions[None, :] < positions[:, None]
    )
    standing = jnp.sum(earlier.astype(jnp.int32), axis=1)
    slot_total = encoders * send_cap
    placing = jnp.where(tissue, tile_encoder * send_cap + standing, slot_total)
    slot_source = jnp.zeros((slot_total,), jnp.int32).at[placing].set(positions, mode="drop")
    outgoing = tiles[tile_rows_of(slot_source)]
    labels = (
        jnp.zeros((slot_total,), jnp.float32)
        .at[placing]
        .set((tile_slot + 1).astype(jnp.float32), mode="drop")
        .astype(jnp.bfloat16)
    )
    arrived, labels_in = (
        lax.all_to_all(
            outgoing.reshape(encoders, send_cap * cells, channels),
            "enc",
            split_axis=0,
            concat_axis=0,
            tiled=True,
        ),
        lax.all_to_all(
            labels.reshape(encoders, send_cap), "enc", split_axis=0, concat_axis=0, tiled=True
        ),
    )
    label_ints = labels_in.reshape(slot_total).astype(jnp.int32)
    filled = label_ints > 0
    seating = jnp.where(filled, label_ints - 1, work_tiles)
    arrival_of = (
        jnp.zeros((work_tiles,), jnp.int32)
        .at[seating]
        .set(jnp.arange(slot_total, dtype=jnp.int32), mode="drop")
    )
    work_batch = arrived.reshape(slot_total * cells, channels)[tile_rows_of(arrival_of)]
    pooled_work = encode_all(work_batch, work_tiles, weights)
    replies = jnp.where(filled[:, None], pooled_work[jnp.minimum(seating, work_tiles - 1)], 0)
    returned = lax.all_to_all(
        replies.reshape(encoders, send_cap, -1), "enc", split_axis=0, concat_axis=0, tiled=True
    )
    pooled = returned.reshape(slot_total, -1)[jnp.minimum(placing, slot_total - 1)]
    counts = slide_counts[0]
    slides = counts.shape[0]
    slide_end = jnp.cumsum(counts)
    slide_start = slide_end - counts
    tile_pos = jnp.arange(tile_total, dtype=jnp.int32)
    member = (
        (tile_pos[None, :] >= slide_start[:, None]) & (tile_pos[None, :] < slide_end[:, None])
    ).astype(jnp.bfloat16)
    sums = jnp.dot(member, pooled, preferred_element_type=jnp.float32)
    means = (sums / jnp.maximum(counts, 1).astype(jnp.float32)[:, None]).astype(jnp.bfloat16)
    owners = slide_owner[:, 0]
    slide_pos = jnp.arange(slides, dtype=jnp.int32)
    before = (owners[None, :] == owners[:, None]) & (slide_pos[None, :] < slide_pos[:, None])
    owner_rank = jnp.sum(before.astype(jnp.int32), axis=1)
    owner_cap = max(2, slides // 2)
    target = owners * owner_cap + owner_rank
    packed = jnp.zeros((loaders * owner_cap, means.shape[1]), jnp.bfloat16).at[target].set(means)
    delivered = lax.all_to_all(
        packed.reshape(loaders, owner_cap, -1), "loader", split_axis=0, concat_axis=0, tiled=True
    )
    return delivered.reshape(loaders * owner_cap, -1)


def solution(mesh):
    placed = (
        P(("loader", "enc"), None),
        P(("loader", "enc")),
        P(("loader", "enc")),
        P(("loader", "enc"), None),
        P(("loader", "enc"), None),
        P(),
        P(),
        P(),
        P(),
        P(),
        P(),
        P(),
        P(),
        P(),
        P(),
        P(),
        P(),
        P(),
    )
    return jax.shard_map(
        body, mesh=mesh, in_specs=placed, out_specs=P(("loader", "enc"), None), check_vma=False
    )
```

profile of v0, /device:TPU:1, one launch (start us, length us, event | category | flops | bytes accessed | tf_op | source)
XLA Modules:
  0.0 282.3 jit_solution(8427180090693016330)
XLA Ops:
  0.0 0.9 convert_reduce_fusion
  0.9 1.2 compare_select_fusion.2
  2.1 0.7 compare_select_fusion.5
  2.8 0.7 scatter_custom_fusion
  3.5 0.7 all_to_all.20
  4.2 7.6 %all-to-all-start = ((bf16[16,1,2]{2,1,0:T(2,128)(2,1)}), bf16[16,1,2]{2,1,0:T(2,128)(2,1)S(1)}, u32[]{:S(2)}, u32[]{:S(2)}) async-start(bf16[16,1,2]{2,1,0:T(2,128)(2,1)} %all_to_all.20), calls=%async_computation | async-start | bytes 16384 | tf_op jit(solution)/shard_map/all_to_all | solution.py:155
  11.8 0.7 scatter_custom_fusion.1
  12.5 0.2 add.461
  12.8 22.6 %gather_fusion = bf16[6272,512]{1,0:T(8,128)(2,1)} fusion(bf16[6272,512]{1,0:T(8,128)(2,1)} %param.20, s32[7168]{0:T(1024)S(1)} %pad_clamp_fusion), kind=kCustom, calls=%fused_computation | custom fusion | bytes 12870144 | tf_op jit(solution)/shard_map/gather | solution.py:140
  35.4 6.8 %all-to-all-start.1 = ((bf16[16,392,512]{2,1,0:T(8,128)(2,1)}), bf16[16,392,512]{2,1,0:T(8,128)(2,1)}, u32[]{:S(2)}, u32[]{:S(2)}) async-start(bf16[16,392,512]{2,1,0:T(8,128)(2,1)} %bitcast.100), calls=%async_computation.1 | async-start | bytes 12845056 | tf_op jit(solution)/shard_map/all_to_all | solution.py:148
  42.3 0.2 reduce-window.7
  42.5 0.2 convert_reduce_fusion.1
  42.7 0.5 fusion.58
  43.2 0.6 bitcast_subtract_fusion
  43.9 0.7 scatter_custom_fusion.2
  44.7 0.1 add.468
  44.9 0.6 copy.46
  45.5 0.6 pad_clamp_fusion.3
  46.2 93.0 %all-to-all-done.1 = bf16[16,392,512]{2,1,0:T(8,128)(2,1)} async-done(((bf16[16,392,512]{2,1,0:T(8,128)(2,1)}), bf16[16,392,512]{2,1,0:T(8,128)(2,1)}, u32[]{:S(2)}, u32[]{:S(2)}) %all-to-all-start.1) | async-done | bytes 6422560 | tf_op jit(solution)/shard_map/all_to_all | solution.py:148
  139.2 14.1 %gather_fusion.1 = bf16[3136,512]{1,0:T(8,128)(2,1)} fusion(bf16[6272,512]{1,0:T(8,128)(2,1)} %bitcast.18, s32[4096]{0:T(1024)S(1)} %pad_clamp_fusion.1), kind=kCustom, calls=%fused_computation.1 | custom fusion | bytes 6435072 | tf_op jit(solution)/shard_map/gather | solution.py:167
  153.4 92.4 %while.12 = (s32[]{:T(128)}, bf16[2,8,1024]{2,1,0:T(8,128)(2,1)S(1)}, f32[256]{0:T(256)S(1)}, f32[256]{0:T(256)S(1)}, bf16[2,1568,512]{2,1,0:T(8,128)(2,1)}, /*i...) while((s32[]{:T(128)}, ...), condition=%wide.region_8.9_spmd, body=%wide.region_6.8_spmd.sunk | while | flops 8253764096 | bytes 152273808 | solution.py:80
  153.6 2.0 fusion.118
  155.6 0.1 dot_general.46
  155.8 0.7 copy.53
  156.5 2.1 fusion.119
  158.7 3.9 %maximum_convert_fusion.6 = bf16[8,196,256]{2,1,0:T(8,128)(2,1)S(1)} fusion(f32[8,196,2304]{2,1,0:T(8,128)S(1)} %fusion.119, f32[256]{0:T(256)S(1)} %get-tuple-element.387, pred[196]{0:T(512)(128)(4,1)S(1)} %get-tuple-element.346, pred[196]{0:T(512)(128)(4,1)S(1)} %get-tuple-element.347, pred[196]{0:T(512)(128)(4,1)S(1)} %compare_and_fusion.6), kind=kLoop, calls=%fused_computation.69.clone.1 | loop fusion | flops 8028160 | bytes 17189376 | tf_op jit(solution)/shard_map/while/body/eval_jaxpr/convert_element_type | solution.py:36
  162.6 1.0 reshape.391
  163.7 3.4 %fusion.117 = f32[1568,1024]{1,0:T(8,128)S(1)} fusion(bf16[512,1024]{1,0:T(8,128)(2,1)S(1)} %copy-done.15, bf16[2,1568,512]{2,1,0:T(8,128)(2,1)} %get-tuple-element.388, s32[]{:T(128)} %get-tuple-element.366), kind=kOutput, calls=%fused_computation.70.clone.1 | convolution fusion | flops 1644167168 | bytes 9077248 | tf_op jit(solution)/shard_map/while/body/eval_jaxpr/dot_general | solution.py:62
  167.1 1.0 maximum_convert_fusion.7
  168.1 1.9 fusion.120
  170.0 2.1 dot_general.47
  172.2 2.4 copy.54
  174.6 3.6 %fusion.121 = f32[8,196,2304]{2,1,0:T(8,128)S(1)} fusion(bf16[8,196,256]{2,1,0:T(8,128)(2,1)} %dot_general.47, bf16[256,2304,1]{0,1,2:T(8,128)(2,1)} %bitcast.97), kind=kOutput, calls=%fused_computation.135.clone.1 | convolution fusion | flops 1849688064 | bytes 16433152 | tf_op jit(solution)/shard_map/while/body/eval_jaxpr/dot_general | solution.py:18
  178.2 4.7 %maximum_convert_fusion.8 = bf16[8,196,256]{2,1,0:T(8,128)(2,1)} fusion(f32[8,196,2304]{2,1,0:T(8,128)S(1)} %fusion.121, f32[256]{0:T(256)S(1)} %get-tuple-element.386, pred[196]{0:T(512)(128)(4,1)S(1)} %get-tuple-element.346, pred[196]{0:T(512)(128)(4,1)S(1)} %get-tuple-element.347, pred[196]{0:T(512)(128)(4,1)S(1)} %compare_and_fusion.6), kind=kLoop, calls=%fused_computation.68.clone.1 | loop fusion | flops 8028160 | bytes 17189376 | tf_op jit(solution)/shard_map/while/body/eval_jaxpr/convert_element_type | solution.py:36
  182.9 2.1 reshape.392
  185.0 5.0 %add_maximum_fusion.2 = f32[1568,1024]{1,0:T(8,128)} fusion(bf16[1568,1024]{1,0:T(8,128)(2,1)S(1)} %maximum_convert_fusion.7, bf16[1568,256]{1,0:T(8,128)(2,1)} %reshape.392, bf16[256,1024]{1,0:T(8,128)(2,1)} %get-tuple-element.398, f32[1024]{0:T(1024)S(1)} %get-tuple-element.399), kind=kOutput, calls=%fused_computation.24.clone.1 | convolution fusion | flops 828506112 | bytes 10964992 | tf_op jit(solution)/shard_map/while/body/eval_jaxpr/dot_general | solution.py:70
  190.0 6.1 %reshape.393 = f32[8,196,1024]{2,1,0:T(8,128)} reshape(f32[1568,1024]{1,0:T(8,128)} %add_maximum_fusion.2) | data formatting | bytes 12845056 | tf_op jit(solution)/shard_map/while/body/eval_jaxpr/reshape | solution.py:74
  196.1 3.6 %reduce_sum.38 = f32[8,1024]{1,0:T(8,128)S(1)} reduce(f32[8,196,1024]{2,1,0:T(8,128)} %reshape.393, f32[]{:T(128)} %constant.101.clone.1..sunk), dimensions={1}, to_apply=%region_7.7 | reduce | flops 1597440 | bytes 6455300 | tf_op jit(solution)/shard_map/while/body/eval_jaxpr/reduce_sum | solution.py:74
  199.7 2.0 fusion.118
  201.7 0.1 dot_general.46
  201.9 0.7 copy.53
  202.6 2.1 fusion.119
  204.8 3.9 %maximum_convert_fusion.6 = bf16[8,196,256]{2,1,0:T(8,128)(2,1)S(1)} fusion(f32[8,196,2304]{2,1,0:T(8,128)S(1)} %fusion.119, f32[256]{0:T(256)S(1)} %get-tuple-element.387, pred[196]{0:T(512)(128)(4,1)S(1)} %get-tuple-element.346, pred[196]{0:T(512)(128)(4,1)S(1)} %get-tuple-element.347, pred[196]{0:T(512)(128)(4,1)S(1)} %compare_and_fusion.6), kind=kLoop, calls=%fused_computation.69.clone.1 | loop fusion | flops 8028160 | bytes 17189376 | tf_op jit(solution)/shard_map/while/body/eval_jaxpr/convert_element_type | solution.py:36
  208.7 1.0 reshape.391
  209.8 3.4 %fusion.117 = f32[1568,1024]{1,0:T(8,128)S(1)} fusion(bf16[512,1024]{1,0:T(8,128)(2,1)S(1)} %copy-done.15, bf16[2,1568,512]{2,1,0:T(8,128)(2,1)} %get-tuple-element.388, s32[]{:T(128)} %get-tuple-element.366), kind=kOutput, calls=%fused_computation.70.clone.1 | convolution fusion | flops 1644167168 | bytes 9077248 | tf_op jit(solution)/shard_map/while/body/eval_jaxpr/dot_general | solution.py:62
  213.2 1.0 maximum_convert_fusion.7
  214.2 1.9 fusion.120
  216.1 2.1 dot_general.47
  218.2 2.4 copy.54
  220.7 3.6 %fusion.121 = f32[8,196,2304]{2,1,0:T(8,128)S(1)} fusion(bf16[8,196,256]{2,1,0:T(8,128)(2,1)} %dot_general.47, bf16[256,2304,1]{0,1,2:T(8,128)(2,1)} %bitcast.97), kind=kOutput, calls=%fused_computation.135.clone.1 | convolution fusion | flops 1849688064 | bytes 16433152 | tf_op jit(solution)/shard_map/while/body/eval_jaxpr/dot_general | solution.py:18
  224.3 4.7 %maximum_convert_fusion.8 = bf16[8,196,256]{2,1,0:T(8,128)(2,1)} fusion(f32[8,196,2304]{2,1,0:T(8,128)S(1)} %fusion.121, f32[256]{0:T(256)S(1)} %get-tuple-element.386, pred[196]{0:T(512)(128)(4,1)S(1)} %get-tuple-element.346, pred[196]{0:T(512)(128)(4,1)S(1)} %get-tuple-element.347, pred[196]{0:T(512)(128)(4,1)S(1)} %compare_and_fusion.6), kind=kLoop, calls=%fused_computation.68.clone.1 | loop fusion | flops 8028160 | bytes 17189376 | tf_op jit(solution)/shard_map/while/body/eval_jaxpr/convert_element_type | solution.py:36
  229.0 2.1 reshape.392
  231.1 5.0 %add_maximum_fusion.2 = f32[1568,1024]{1,0:T(8,128)} fusion(bf16[1568,1024]{1,0:T(8,128)(2,1)S(1)} %maximum_convert_fusion.7, bf16[1568,256]{1,0:T(8,128)(2,1)} %reshape.392, bf16[256,1024]{1,0:T(8,128)(2,1)} %get-tuple-element.398, f32[1024]{0:T(1024)S(1)} %get-tuple-element.399), kind=kOutput, calls=%fused_computation.24.clone.1 | convolution fusion | flops 828506112 | bytes 10964992 | tf_op jit(solution)/shard_map/while/body/eval_jaxpr/dot_general | solution.py:70
  236.0 6.1 %reshape.393 = f32[8,196,1024]{2,1,0:T(8,128)} reshape(f32[1568,1024]{1,0:T(8,128)} %add_maximum_fusion.2) | data formatting | bytes 12845056 | tf_op jit(solution)/shard_map/while/body/eval_jaxpr/reshape | solution.py:74
  242.2 3.6 %reduce_sum.38 = f32[8,1024]{1,0:T(8,128)S(1)} reduce(f32[8,196,1024]{2,1,0:T(8,128)} %reshape.393, f32[]{:T(128)} %constant.101.clone.1..sunk), dimensions={1}, to_apply=%region_7.7 | reduce | flops 1597440 | bytes 6455300 | tf_op jit(solution)/shard_map/while/body/eval_jaxpr/reduce_sum | solution.py:74
  245.8 0.8 gather_fusion.2
  246.6 0.8 broadcast_select_fusion
  247.4 11.9 %all-to-all-start.2 = ((bf16[16,2,1024]{2,1,0:T(2,128)(2,1)}), bf16[16,2,1024]{2,1,0:T(2,128)(2,1)S(1)}, u32[]{:S(2)}, u32[]{:S(2)}) async-start(bf16[16,2,1024]{2,1,0:T(2,128)(2,1)} %broadcast_select_fusion), calls=%async_computation.2 | async-start | bytes 131072 | tf_op jit(solution)/shard_map/all_to_all | solution.py:170
  259.3 6.5 %all-to-all-done.2 = bf16[16,2,1024]{2,1,0:T(2,128)(2,1)S(1)} async-done(((bf16[16,2,1024]{2,1,0:T(2,128)(2,1)}), bf16[16,2,1024]{2,1,0:T(2,128)(2,1)S(1)}, u32[]{:S(2)}, u32[]{:S(2)}) %all-to-all-start.2) | async-done | bytes 65568 | tf_op jit(solution)/shard_map/all_to_all | solution.py:170
  265.9 0.6 gather_fusion.3
  266.5 0.2 fusion.47
  266.7 0.8 scatter_custom_fusion.3
  267.5 14.1 %all_to_all.25 = bf16[8,4,1024]{2,1,0:T(4,128)(2,1)S(1)} all-to-all(bf16[8,4,1024]{2,1,0:T(4,128)(2,1)S(1)} %reshape.300), channel_id=1, replica_groups=mesh['loader'=8,'enc'=16] {'loader'}, dimensions={0} | all-to-all | bytes 131072 | tf_op jit(solution)/shard_map/all_to_all | solution.py:191
  281.6 0.6 reshape.301
  (80 shorter events, 0.9 us)
Async XLA Ops:
  4.2 31.3 %all-to-all-start = ((bf16[16,1,2]{2,1,0:T(2,128)(2,1)}), bf16[16,1,2]{2,1,0:T(2,128)(2,1)S(1)}, u32[]{:S(2)}, u32[]{:S(2)}) async-start(bf16[16,1,2]{2,1,0:T(2,128)(2,1)} %all_to_all.20), calls=%async_computation | async-start | bytes 16384 | tf_op jit(solution)/shard_map/all_to_all | solution.py:155
  35.4 6.9 %copy-start.10 = (s32[1,8]{1,0:T(1,128)S(1)}, s32[1,8]{1,0:T(1,128)}, u32[]{:S(2)}) copy-start(s32[1,8]{1,0:T(1,128)} %param.23) | copy-start | bytes 100
  35.4 7.1 %copy-start.20 = (s32[8,1]{0,1:T(1,128)S(1)}, s32[8,1]{0,1:T(1,128)}, u32[]{:S(2)}) copy-start(s32[8,1]{0,1:T(1,128)} %param.24) | copy-start | bytes 100
  35.4 103.7 %all-to-all-start.1 = ((bf16[16,392,512]{2,1,0:T(8,128)(2,1)}), bf16[16,392,512]{2,1,0:T(8,128)(2,1)}, u32[]{:S(2)}, u32[]{:S(2)}) async-start(bf16[16,392,512]{2,1,0:T(8,128)(2,1)} %bitcast.100), calls=%async_computation.1 | async-start | bytes 12845056 | tf_op jit(solution)/shard_map/all_to_all | solution.py:148
  42.5 0.7 copy-start.11
  139.2 14.2 %copy-start.1 = (bf16[2304,256]{1,0:T(8,128)(2,1)S(1)}, bf16[2304,256]{1,0:T(8,128)(2,1)}, u32[]{:S(2)}) copy-start(bf16[2304,256]{1,0:T(8,128)(2,1)} %param.27) | copy-start | bytes 3538948
  139.2 14.2 %copy-start.4 = (f32[1024]{0:T(1024)S(1)}, f32[1024]{0:T(1024)}, u32[]{:S(2)}) copy-start(f32[1024]{0:T(1024)} %param.37) | copy-start | bytes 12292
  139.2 14.2 %copy-start.5 = (f32[1024]{0:T(1024)S(1)}, f32[1024]{0:T(1024)}, u32[]{:S(2)}) copy-start(f32[1024]{0:T(1024)} %param.31) | copy-start | bytes 12292
  139.2 14.2 %copy-start.6 = (f32[256]{0:T(256)S(1)}, f32[256]{0:T(256)}, u32[]{:S(2)}) copy-start(f32[256]{0:T(256)} %param.35) | copy-start | bytes 3076
  139.2 14.2 %copy-start.7 = (f32[256]{0:T(256)S(1)}, f32[256]{0:T(256)}, u32[]{:S(2)}) copy-start(f32[256]{0:T(256)} %param.28) | copy-start | bytes 3076
  139.2 14.2 %copy-start.17 = (bf16[512,256]{1,0:T(8,128)(2,1)S(1)}, bf16[512,256]{1,0:T(8,128)(2,1)}, u32[]{:S(2)}) copy-start(bf16[512,256]{1,0:T(8,128)(2,1)} %param.25) | copy-start | bytes 786436
  139.2 14.2 %copy-start.18 = (f32[256]{0:T(256)S(1)}, f32[256]{0:T(256)}, u32[]{:S(2)}) copy-start(f32[256]{0:T(256)} %param.26) | copy-start | bytes 3076
  139.2 14.2 %copy-start.19 = (f32[256]{0:T(256)S(1)}, f32[256]{0:T(256)}, u32[]{:S(2)}) copy-start(f32[256]{0:T(256)} %param.33) | copy-start | bytes 3076
  153.4 93.2 %copy-start.8 = (pred[16,2]{1,0:T(8,128)(4,1)S(1)}, pred[16,2]{1,0:T(8,128)(4,1)}, u32[]{:S(2)}) copy-start(pred[16,2]{1,0:T(8,128)(4,1)} %copy.46) | copy-start | bytes 100
  153.4 105.9 %copy-start.9 = (s32[32]{0:T(128)S(1)}, s32[32]{0:T(128)}, u32[]{:S(2)}) copy-start(s32[32]{0:T(128)} %get-tuple-element.237) | copy-start | bytes 388
  158.7 5.0 %copy-start.15 = (bf16[512,1024]{1,0:T(8,128)(2,1)S(1)}, bf16[512,1024]{1,0:T(8,128)(2,1)}, u32[]{:S(2)}) copy-start(bf16[512,1024]{1,0:T(8,128)(2,1)} %get-tuple-element.393) | copy-start | bytes 3145732 | tf_op jit(solution)/shard_map/while
  163.7 3.4 %copy-start = (bf16[1568,256]{1,0:T(8,128)(2,1)S(1)}, bf16[1568,256]{1,0:T(8,128)(2,1)}, u32[]{:S(2)}) copy-start(bf16[1568,256]{1,0:T(8,128)(2,1)} %reshape.391) | copy-start | bytes 2408452 | tf_op jit(solution)/shard_map/while
  163.7 3.4 %copy-start.3 = (bf16[256,1024]{1,0:T(8,128)(2,1)S(1)}, bf16[256,1024]{1,0:T(8,128)(2,1)}, u32[]{:S(2)}) copy-start(bf16[256,1024]{1,0:T(8,128)(2,1)} %get-tuple-element.392) | copy-start | bytes 1572868 | tf_op jit(solution)/shard_map/while
  167.1 1.0 copy-start.16
  196.1 3.6 %copy-start.2 = (bf16[2304,256]{1,0:T(8,128)(2,1)S(1)}, bf16[2304,256]{1,0:T(8,128)(2,1)}, u32[]{:S(2)}) copy-start(bf16[2304,256]{1,0:T(8,128)(2,1)} %get-tuple-element.420) | copy-start | bytes 3538948 | tf_op jit(solution)/shard_map/while
  204.8 5.0 %copy-start.15 = (bf16[512,1024]{1,0:T(8,128)(2,1)S(1)}, bf16[512,1024]{1,0:T(8,128)(2,1)}, u32[]{:S(2)}) copy-start(bf16[512,1024]{1,0:T(8,128)(2,1)} %get-tuple-element.393) | copy-start | bytes 3145732 | tf_op jit(solution)/shard_map/while
  209.8 3.4 %copy-start = (bf16[1568,256]{1,0:T(8,128)(2,1)S(1)}, bf16[1568,256]{1,0:T(8,128)(2,1)}, u32[]{:S(2)}) copy-start(bf16[1568,256]{1,0:T(8,128)(2,1)} %reshape.391) | copy-start | bytes 2408452 | tf_op jit(solution)/shard_map/while
  209.8 3.4 %copy-start.3 = (bf16[256,1024]{1,0:T(8,128)(2,1)S(1)}, bf16[256,1024]{1,0:T(8,128)(2,1)}, u32[]{:S(2)}) copy-start(bf16[256,1024]{1,0:T(8,128)(2,1)} %get-tuple-element.392) | copy-start | bytes 1572868 | tf_op jit(solution)/shard_map/while
  213.2 1.0 copy-start.16
  242.2 3.6 %copy-start.2 = (bf16[2304,256]{1,0:T(8,128)(2,1)S(1)}, bf16[2304,256]{1,0:T(8,128)(2,1)}, u32[]{:S(2)}) copy-start(bf16[2304,256]{1,0:T(8,128)(2,1)} %get-tuple-element.420) | copy-start | bytes 3538948 | tf_op jit(solution)/shard_map/while
  245.8 20.7 %copy-start.12 = (s32[8,1]{0,1:T(1,128)S(1)}, s32[8,1]{0,1:T(1,128)}, u32[]{:S(2)}) copy-start(s32[8,1]{0,1:T(1,128)} %copy-done.11) | copy-start | bytes 100
  245.8 20.7 %copy-start.13 = (s32[8]{0:T(128)S(1)}, s32[8]{0:T(128)}, u32[]{:S(2)}) copy-start(s32[8]{0:T(128)} %get-tuple-element.241) | copy-start | bytes 100
  245.8 20.7 %copy-start.14 = (f32[8]{0:T(128)S(1)}, f32[8]{0:T(128)}, u32[]{:S(2)}) copy-start(f32[8]{0:T(128)} %get-tuple-element.242) | copy-start | bytes 100
  247.4 18.4 %all-to-all-start.2 = ((bf16[16,2,1024]{2,1,0:T(2,128)(2,1)}), bf16[16,2,1024]{2,1,0:T(2,128)(2,1)S(1)}, u32[]{:S(2)}, u32[]{:S(2)}) async-start(bf16[16,2,1024]{2,1,0:T(2,128)(2,1)} %broadcast_select_fusion), calls=%async_computation.2 | async-start | bytes 131072 | tf_op jit(solution)/shard_map/all_to_all | solution.py:170
where the time goes:
time: 283 us; the launch traced here: 282 us
  waiting for transfers between devices  99.5 us (35%)
  local copies, waits for them, and re-layouts  73.1 us (26%)
  matrix products  38.2 us (13%)
  other arithmetic  30.4 us (11%)
  starting transfers between devices  26.3 us (9%)
  blocking collectives  14.1 us (5%)
    all_to_all x1, waiting for transfers between devices, body(): lax.all_to_all(outgoing.reshape(encoders, send_cap * cells, channels), 'e...  93 us
    gather x1, local copies, waits for them, and re-layouts, body(): outgoing = tiles[tile_rows_of(slot_source)]  22.6 us
    convert_element_type x4, other arithmetic, spatial_conv(): jax.nn.relu(summed).astype(jnp.bfloat16)  17.2 us
    gather x1, local copies, waits for them, and re-layouts, body(): arrived.reshape(slot_total * cells, channels)[tile_rows_of(arrival_of)]  14.1 us
    all_to_all x1, blocking collectives, body(): lax.all_to_all(packed.reshape(loaders, owner_cap, -1), 'loader', split_ax...  14.1 us
    reshape x2, local copies, waits for them, and re-layouts, encode(): block_out.reshape(tile_count, GRID * GRID, -1)  12.3 us
    all_to_all x1, starting transfers between devices, body(): lax.all_to_all(replies.reshape(encoders, send_cap, -1), 'enc', split_axis...  11.9 us
    dot_general x4, matrix products, spatial_conv(): jnp.dot(flat_rows, tap_weights, preferred_element_type=jnp.float32)  11.5 us
  transfers between devices with their start and end apart: 3, of which 2 were waited for; matrix products, arithmetic and copies ran while one was open for 10% of the time, Pallas kernels for 0%

commit v1 on v0

v1 whole, which is shorter than its diff:
```python
import functools

import jax
import jax.numpy as jnp
from jax import lax
from jax.experimental import pallas as pl
from jax.experimental.pallas import tpu as pltpu
from jax.sharding import PartitionSpec as P

GRID = 14
CELLS = GRID * GRID
BATCH = 16
ROWS = BATCH * CELLS
STEP = 2
CHUNK = STEP * GRID * BATCH


def encoder_kernel(
    slide_end,
    slide_count,
    owner,
    b_reduce,
    b_spatial,
    b_join,
    b_reduce2,
    b_spatial2,
    b_expand2,
    tiles,
    w_reduce_hbm,
    w_spatial_hbm,
    w_expand_hbm,
    w_short_hbm,
    w_reduce2_hbm,
    w_spatial2_hbm,
    w_expand2_hbm,
    out,
    w_reduce,
    w_spatial,
    w_join,
    w_reduce2,
    w_spatial2,
    w_expand2,
    arrived,
    spread_out,
    pixels,
    reduced,
    narrowed,
    joined,
    pooled,
    weight_sem,
    tile_sem,
):
    f32, bf16 = jnp.float32, jnp.bfloat16
    slides = slide_count.shape[1]
    tissue = slide_end[0, slides - 1]
    mid = w_expand_hbm.shape[0]
    batches = arrived.shape[0]

    def tile_copy(batch):
        return pltpu.make_async_copy(
            tiles.at[pl.ds(batch * ROWS, ROWS)], arrived.at[batch], tile_sem.at[batch]
        )

    tile_copy(0).start()
    moves = [
        (w_reduce_hbm, w_reduce),
        (w_spatial_hbm, w_spatial),
        (w_expand_hbm, w_join.at[pl.ds(0, mid)]),
        (w_short_hbm, w_join.at[pl.ds(mid, w_short_hbm.shape[0])]),
        (w_reduce2_hbm, w_reduce2),
        (w_spatial2_hbm, w_spatial2),
        (w_expand2_hbm, w_expand2),
    ]
    copies = [
        pltpu.make_async_copy(source, target, weight_sem.at[index])
        for index, (source, target) in enumerate(moves)
    ]
    for copy in copies:
        copy.start()
    for batch in range(1, batches):
        tile_copy(batch).start()

    reduced[...] = jnp.zeros_like(reduced)
    narrowed[...] = jnp.zeros_like(narrowed)
    pooled[...] = jnp.zeros_like(pooled)

    def window(padded, first):
        pieces = [
            padded[pl.ds(first + a, STEP), b : b + GRID, :, :].reshape(CHUNK, mid)
            for a in range(3)
            for b in range(3)
        ]
        return jnp.concatenate(pieces, axis=1)

    def encode(batch):
        def widen(step, _):
            rows = pl.ds(pl.multiple_of(step * CHUNK, CHUNK), CHUNK)
            block = arrived[batch, rows, :].astype(f32)
            for lane in range(4):
                spread_out[lane, rows, :] = block[:, lane * 128 : (lane + 1) * 128]
            return 0

        lax.fori_loop(0, ROWS // CHUNK, widen, 0)

        def turn(row, _):
            for column in range(GRID):
                place = row * GRID + column
                for lane in range(4):
                    piece = spread_out[lane, pl.ds(place, BATCH, stride=CELLS), :]
                    pixels[
                        pl.ds(pl.multiple_of(place * BATCH, BATCH), BATCH),
                        lane * 128 : (lane + 1) * 128,
                    ] = piece.astype(bf16)
            return 0

        lax.fori_loop(0, GRID, turn, 0)

        def first(step, _):
            rows = pl.ds(pl.multiple_of(step * CHUNK, CHUNK), CHUNK)
            value = jnp.dot(pixels[rows, :], w_reduce[...], preferred_element_type=f32)
            value = jnp.maximum(value + b_reduce[...], 0.0).astype(bf16)
            reduced[pl.ds(step * STEP + 1, STEP), 1 : GRID + 1, :, :] = value.reshape(
                STEP, GRID, BATCH, mid
            )
            return 0

        lax.fori_loop(0, GRID // STEP, first, 0)

        def second(step, _):
            rows = pl.ds(pl.multiple_of(step * CHUNK, CHUNK), CHUNK)
            spatial = jnp.dot(
                window(reduced, step * STEP), w_spatial[...], preferred_element_type=f32
            )
            spatial = jnp.maximum(spatial + b_spatial[...], 0.0).astype(bf16)
            both = jnp.concatenate([spatial, pixels[rows, :]], axis=1)
            value = jnp.dot(both, w_join[...], preferred_element_type=f32)
            value = jnp.maximum(value + b_join[...], 0.0).astype(bf16)
            joined[rows, :] = value
            value = jnp.dot(value, w_reduce2[...], preferred_element_type=f32)
            value = jnp.maximum(value + b_reduce2[...], 0.0).astype(bf16)
            narrowed[pl.ds(step * STEP + 1, STEP), 1 : GRID + 1, :, :] = value.reshape(
                STEP, GRID, BATCH, mid
            )
            return 0

        lax.fori_loop(0, GRID // STEP, second, 0)

        def third(step, total):
            rows = pl.ds(pl.multiple_of(step * CHUNK, CHUNK), CHUNK)
            spread = jnp.dot(
                window(narrowed, step * STEP), w_spatial2[...], preferred_element_type=f32
            )
            spread = jnp.maximum(spread + b_spatial2[...], 0.0).astype(bf16)
            value = jnp.dot(spread, w_expand2[...], preferred_element_type=f32)
            value = jnp.maximum(value + b_expand2[...] + joined[rows, :].astype(f32), 0.0)
            return total + jnp.sum(value.reshape(STEP * GRID, BATCH, -1), axis=0)

        total = lax.fori_loop(
            0, GRID // STEP, third, jnp.zeros((BATCH, joined.shape[1]), f32)
        )
        pooled[batch * BATCH : (batch + 1) * BATCH, :] = (total / CELLS).astype(bf16)

    for batch in range(batches):
        tile_copy(batch).wait()
        if batch == 0:
            for copy in copies:
                copy.wait()
        pl.when(tissue > batch * BATCH)(functools.partial(encode, batch))

    received = out.shape[0]
    shape = (received, pooled.shape[0])
    row = lax.broadcasted_iota(jnp.int32, shape, 0)
    place = lax.broadcasted_iota(jnp.int32, shape, 1)
    row_only = lax.broadcasted_iota(jnp.int32, (received, 1), 0)
    chosen = jnp.zeros(shape, f32)
    divisor = jnp.ones((received, 1), f32)
    cap = received // 8
    for j in range(slides):
        standing = jnp.int32(0)
        for earlier in range(j):
            standing += (owner[earlier, 0] == owner[j, 0]).astype(jnp.int32)
        target = owner[j, 0] * cap + standing
        end, count = slide_end[0, j], slide_count[0, j]
        member = (row == target) & (place >= end - count) & (place < end)
        chosen = jnp.where(member, 1.0, chosen)
        size = jnp.maximum(count, 1).astype(f32)
        divisor = jnp.where(row_only == target, size, divisor)
    sums = jnp.dot(chosen.astype(bf16), pooled[...], preferred_element_type=f32)
    out[...] = (sums / divisor).astype(bf16)


def body(
    tiles,
    tile_encoder,
    tile_slot,
    slide_counts,
    slide_owner,
    w_reduce,
    b_reduce,
    w_spatial,
    b_spatial,
    w_expand,
    w_short,
    b_join,
    w_reduce2,
    b_reduce2,
    w_spatial2,
    b_spatial2,
    w_expand2,
    b_expand2,
):
    bf16, f32 = jnp.bfloat16, jnp.float32
    places = tile_encoder.shape[0]
    loaders = lax.axis_size("loader")
    c_in, c_mid = w_reduce.shape
    c_out = w_expand.shape[1]
    batches = places // BATCH
    slide_end = jnp.cumsum(slide_counts, axis=1)
    smem = pl.BlockSpec(memory_space=pltpu.SMEM)
    vmem = pl.BlockSpec(memory_space=pltpu.VMEM)
    anywhere = pl.BlockSpec(memory_space=pl.ANY)
    packed = pl.pallas_call(
        encoder_kernel,
        out_shape=jax.ShapeDtypeStruct((places, c_out), bf16),
        in_specs=[smem] * 3 + [vmem] * 6 + [anywhere] * 8,
        out_specs=vmem,
        scratch_shapes=[
            pltpu.VMEM(w_reduce.shape, bf16),
            pltpu.VMEM(w_spatial.shape, bf16),
            pltpu.VMEM((c_mid + c_in, c_out), bf16),
            pltpu.VMEM(w_reduce2.shape, bf16),
            pltpu.VMEM(w_spatial2.shape, bf16),
            pltpu.VMEM(w_expand2.shape, bf16),
            pltpu.VMEM((batches, ROWS, c_in), bf16),
            pltpu.VMEM((4, ROWS, 128), f32),
            pltpu.VMEM((ROWS, c_in), bf16),
            pltpu.VMEM((GRID + 2, GRID + 2, BATCH, c_mid), bf16),
            pltpu.VMEM((GRID + 2, GRID + 2, BATCH, c_mid), bf16),
            pltpu.VMEM((ROWS, c_out), bf16),
            pltpu.VMEM((places, c_out), bf16),
            pltpu.SemaphoreType.DMA((7,)),
            pltpu.SemaphoreType.DMA((batches,)),
        ],
        compiler_params=pltpu.CompilerParams(vmem_limit_bytes=60 * 1024 * 1024),
        name="encode_tiles",
    )(
        slide_end,
        slide_counts,
        slide_owner,
        b_reduce[None],
        b_spatial[None],
        b_join[None],
        b_reduce2[None],
        b_spatial2[None],
        b_expand2[None],
        tiles,
        w_reduce,
        w_spatial,
        w_expand,
        w_short,
        w_reduce2,
        w_spatial2,
        w_expand2,
    )
    delivered = lax.all_to_all(
        packed.reshape(loaders, places // loaders, -1),
        "loader",
        split_axis=0,
        concat_axis=0,
        tiled=True,
    )
    return delivered.reshape(places, -1)


def solution(mesh):
    split = P(("loader", "enc"))
    placed = (split,) * 5 + (P(),) * 13
    return jax.shard_map(
        body, mesh=mesh, in_specs=placed, out_specs=split, check_vma=False
    )
```

time: 283 us -> 85.6 us (0.30)
  waiting for transfers between devices: 99.5 us -> 0 us
  local copies, waits for them, and re-layouts: 73.1 us -> 2.84 us
  Pallas kernels: 0 us -> 69.7 us
  matrix products: 38.2 us -> 0 us
  other arithmetic: 30.4 us -> 1.33 us
  starting transfers between devices: 26.3 us -> 0 us
    all_to_all x3 -> x0, waiting for transfers between devices: 99.5 us -> none  [the longest x1 93 us: body(): lax.all_to_all(outgoing.reshape(encoders, send_cap * cells, channels), 'e...]
    pallas_call x0 -> x1, Pallas kernels: none -> 69.7 us  [body(): pl.pallas_call(encoder_kernel, out_shape=jax.ShapeDtypeStruct((places, c_...]
    gather x5 -> x0, local copies, waits for them, and re-layouts: 38.2 us -> none  [the longest x1 22.6 us: body(): outgoing = tiles[tile_rows_of(slot_source)]]
    dot_general x15 -> x0, matrix products: 38.2 us -> none  [the longest x4 11.5 us: spatial_conv(): jnp.dot(flat_rows, tap_weights, preferred_element_type=jnp.float32)]
    all_to_all x3 -> x0, starting transfers between devices: 26.3 us -> none  [the longest x1 11.9 us: body(): lax.all_to_all(replies.reshape(encoders, send_cap, -1), 'enc', split_axis...]
    reshape x9 -> x2, local copies, waits for them, and re-layouts: 19.3 us -> 1.52 us  [the longest x1 0.87 us: body(): packed.reshape(loaders, places // loaders, -1)]
    convert_element_type x5 -> x0, other arithmetic: 17.2 us -> none  [the longest x4 17.2 us: spatial_conv(): jax.nn.relu(summed).astype(jnp.bfloat16)]
    reduce_sum x4 -> x0, other arithmetic: 8.24 us -> none  [the longest x2 7.16 us: encode(): jnp.mean(block_out.reshape(tile_count, GRID * GRID, -1), axis=1)]
  transfers between devices with their start and end apart: 3 -> 0, of which waited for: 2 -> 0; matrix products, arithmetic and copies ran while one was open for 10% -> 0% of each run, Pallas kernels for 0% -> 0%
where the time goes in v1:
time: 85.6 us; the launch traced here: 85.3 us
  Pallas kernels  69.7 us (81%)
  blocking collectives  11.5 us (13%)
  local copies, waits for them, and re-layouts  2.84 us (3%)
  other arithmetic  1.33 us (2%)
    pallas_call x1, Pallas kernels, body(): pl.pallas_call(encoder_kernel, out_shape=jax.ShapeDtypeStruct((places, c_...  69.7 us
    all_to_all x1, blocking collectives, body(): lax.all_to_all(packed.reshape(loaders, places // loaders, -1), 'loader',...  11.5 us

profile of v1, /device:TPU:1, one launch (start us, length us, event | category | flops | bytes accessed | tf_op | source)
XLA Modules:
  0.0 85.3 jit_solution(75321818452054688)
XLA Ops:
  0.0 1.3 %copy.17.owner = s32[8,1]{1,0:T(8,128)} copy(s32[8,1]{0,1:T(1,128)} %param.20) | data formatting | bytes 64 | tf_op args[4]
  1.3 1.3 %reduce_window_sum.11.slide_end = s32[1,8]{1,0:T(1,128)} reduce-window(s32[1,8]{1,0:T(1,128)} %slide_count.1, s32[]{:T(128)} %constant.3.clone.1), window={size=1x8 pad=0_0x7_0}, to_apply=%region_0.0 | reduce-window | flops 56 | bytes 68 | tf_op jit(solution)/shard_map/jit(cumsum)/reduce_window_sum | solution.py:218
  2.6 69.7 %encode_tiles.1 = bf16[32,1024]{1,0:T(8,128)(2,1)} custom-call(s32[1,8]{1,0:T(1,128)} %reduce_window_sum.11.slide_end, s32[1,8]{1,0:T(1,128)} %slide_count.1, s32[8,1]{1,0:T(8,128)} %copy.17.owner, f32[1,256]{1,0:T(1,128)} %bitcast.8, f32[1,256]{1,0:T(1,128)} %bitcast.9, f32[1,1024]{1,0:T(1,128)} %bitcast.6, f32[1,256]{1,0:T(1,128)} %bitcast.10, ...), custom_call_target="tpu_custom_call" | custom-call | tf_op jit(solution)/shard_map/encode_tiles/pallas_call | solution.py:222
  72.3 0.9 %reshape.6 = bf16[8,4,1024]{2,1,0:T(4,128)(2,1)S(1)} reshape(bf16[32,1024]{1,0:T(8,128)(2,1)} %encode_tiles.1) | data formatting | bytes 131072 | tf_op jit(solution)/shard_map/reshape | solution.py:266
  73.2 11.5 %all_to_all.5 = bf16[8,4,1024]{2,1,0:T(4,128)(2,1)S(1)} all-to-all(bf16[8,4,1024]{2,1,0:T(4,128)(2,1)S(1)} %reshape.6), channel_id=1, replica_groups=mesh['loader'=8,'enc'=16] {'loader'}, dimensions={0} | all-to-all | bytes 131072 | tf_op jit(solution)/shard_map/all_to_all | solution.py:265
  84.7 0.6 reshape.7

commit v2 on v1

v2 whole, which is shorter than its diff:
```python
import functools

import jax
import jax.numpy as jnp
from jax import lax
from jax.experimental import pallas as pl
from jax.experimental.pallas import tpu as pltpu
from jax.sharding import PartitionSpec as P

MESH = pl.DeviceIdType.MESH
GRID = 14
CELLS = GRID * GRID
BATCH = 8
ROWS = BATCH * CELLS
LINE = GRID * BATCH
PAIRS = GRID // 2 + 1


def encoder_kernel(
    counts_ref,
    owner_ref,
    b_reduce,
    b_spatial,
    b_join,
    b_reduce2,
    b_spatial2,
    b_expand2,
    tiles,
    w_reduce_hbm,
    w_spatial_hbm,
    w_expand_hbm,
    w_short_hbm,
    w_reduce2_hbm,
    w_spatial2_hbm,
    w_expand2_hbm,
    out,
    w_reduce,
    w_spatial,
    w_join,
    w_reduce2,
    w_spatial2,
    w_expand2,
    arrived,
    widened,
    pixels,
    reduced_even,
    reduced_odd,
    narrowed_even,
    narrowed_odd,
    spatial,
    joined,
    residual,
    pooled,
    weight_sem,
    tile_sem,
):
    f32, bf16 = jnp.float32, jnp.bfloat16
    slides = counts_ref.shape[1]
    mid = w_expand_hbm.shape[0]
    most = arrived.shape[0]
    counts = [counts_ref[0, j] for j in range(slides)]
    ends = [counts[0]]
    for count in counts[1:]:
        ends.append(ends[-1] + count)
    batches = (ends[-1] + BATCH - 1) // BATCH

    def tile_copy(batch):
        rows = pl.ds(pl.multiple_of(batch * ROWS, ROWS), ROWS)
        return pltpu.make_async_copy(tiles.at[rows], arrived.at[batch], tile_sem.at[batch])

    moves = [
        (w_reduce_hbm, w_reduce),
        (w_spatial_hbm, w_spatial),
        (w_expand_hbm, w_join.at[pl.ds(0, mid)]),
        (w_short_hbm, w_join.at[pl.ds(mid, w_short_hbm.shape[0])]),
        (w_reduce2_hbm, w_reduce2),
        (w_spatial2_hbm, w_spatial2),
        (w_expand2_hbm, w_expand2),
    ]
    copies = [
        pltpu.make_async_copy(source, target, weight_sem.at[index])
        for index, (source, target) in enumerate(moves)
    ]
    pl.when(batches > 0)(lambda: tile_copy(0).start())
    for copy in copies:
        copy.start()
    for batch in range(1, most):
        pl.when(batches > batch)(functools.partial(lambda b: tile_copy(b).start(), batch))

    border = jnp.zeros((1,) + reduced_even.shape[1:], bf16)
    for padded in (reduced_even, reduced_odd, narrowed_even, narrowed_odd):
        padded[0:1] = border
        padded[GRID + 1 : GRID + 2] = border
    pooled[...] = jnp.zeros_like(pooled)

    half = GRID // 2
    order = [(lane, k) for k in range(half) for lane in range(2)]

    def image_row(mxu, k):
        return k if mxu == 0 else GRID - 1 - k

    def keep(even, odd, bias):
        def finish(i, n, value):
            value = jnp.maximum(value + bias[...], 0.0).reshape(GRID, BATCH, mid)
            side = jnp.zeros((1, BATCH, mid), f32)
            whole = jnp.concatenate([side, value, side], axis=0)
            even[i + 1] = whole.reshape(PAIRS, 2 * BATCH, mid).astype(bf16)
            odd[i + 1, 0 : PAIRS - 1] = value.reshape(
                PAIRS - 1, 2 * BATCH, mid
            ).astype(bf16)

        return finish

    def tap(even, odd):
        def left(i, k):
            a, b = k // 3, k % 3
            source = odd if b == 1 else even
            first = 1 if b == 2 else 0
            piece = source[i + a, first : first + PAIRS - 1]
            return piece.reshape(LINE, mid)

        return left

    def line(i):
        return slice(i * LINE, (i + 1) * LINE)

    def lanes(n):
        return slice(n * mid, (n + 1) * mid)

    def plain(target, bias):
        def finish(i, n, value):
            value = jnp.maximum(value + bias[:, lanes(n)], 0.0).astype(bf16)
            target[line(i), lanes(n)] = value

        return finish

    def join(i, n, value):
        value = jnp.maximum(value + b_join[:, lanes(n)], 0.0)
        joined[line(i), lanes(n)] = value.astype(bf16)
        residual[line(i), lanes(n)] = value + b_expand2[:, lanes(n)]

    def tiles_of(ref):
        return lambda i, k: ref[line(i), lanes(k)]

    def run(stages, *accs):
        passes = []
        for left, weights, finish, lag, beside in stages:
            depth, width = weights.shape[0] // mid, weights.shape[1] // mid
            for n in range(width):
                for k in range(depth):
                    ahead = lag if n == 0 else 0
                    passes.append((left, weights, finish, n, k, k == depth - 1, ahead, beside))

        def push(index):
            _, weights, _, n, k, _, _, _ = passes[index]
            for mxu in range(2):
                pltpu.matmul_push_rhs(
                    weights[lanes(k), lanes(n)], staging_register=index % 2, mxu_index=mxu
                )

        def pop(finish, n, k):
            for mxu in range(2):
                finish(image_row(mxu, k), n, pltpu.matmul_pop(accs[mxu * half + k]))

        push(0)
        waiting = None
        for index, (left, weights, finish, n, k, last, lag, beside) in enumerate(passes):
            if index + 1 < len(passes):
                push(index + 1)
            popped = 0
            for block in range(half):
                if beside is not None:
                    beside(k * half + block)
                if waiting is not None:
                    while popped < min(half, block + 1 + lag):
                        pop(*waiting, popped)
                        popped += 1
                for mxu in range(2):
                    pltpu.matmul_acc_lhs(
                        accs[mxu * half + block],
                        left(image_row(mxu, block), k),
                        load_staged_rhs=index % 2 if block == 0 else None,
                    )
            waiting = (finish, n) if last else None
        for block in range(half):
            pop(*waiting, block)

    def widen(batch, i):
        block = arrived[batch, line(i), :].astype(f32)
        for lane in range(4):
            widened[lane, line(i), :] = block[:, lane * 128 : (lane + 1) * 128]

    def turn(pair):
        for lane in range(4):
            two = [
                widened[lane, pl.ds(2 * pair + k, BATCH, stride=CELLS), :] for k in range(2)
            ]
            pixels[
                pair * 2 * BATCH : (pair + 1) * 2 * BATCH, lane * 128 : (lane + 1) * 128
            ] = jnp.concatenate(two, axis=0).astype(bf16)

    @pl.when(batches > 0)
    def _():
        tile_copy(0).wait()
        for i in range(GRID):
            widen(0, i)
        for pair in range(CELLS // 2):
            turn(pair)

    for copy in copies:
        copy.wait()

    def encode(batch, _):
        pl.when(batch + 1 < batches)(lambda: tile_copy(batch + 1).wait())
        following = jnp.minimum(batch + 1, most - 1)
        totals = {}

        def widen_next(step):
            if step % 4 == 0 and step // 4 < GRID:
                widen(following, step // 4)

        def turn_next(step):
            for pair in (2 * step, 2 * step + 1):
                if pair < CELLS // 2:
                    turn(pair)

        def pool(i, n, value):
            value = jnp.maximum(value + residual[line(i), lanes(n)], 0.0)
            value = value.reshape(GRID, BATCH, mid)
            value = jnp.sum(value, axis=0)
            totals[n] = totals[n] + value if n in totals else value

        def both(i, k):
            if k == 0:
                return spatial[line(i), :]
            return pixels[line(i), lanes(k - 1)]

        stages = [
            (tiles_of(pixels), w_reduce, keep(reduced_even, reduced_odd, b_reduce), 0, None),
            (tap(reduced_even, reduced_odd), w_spatial, plain(spatial, b_spatial), 1, widen_next),
            (both, w_join, join, 1, None),
            (tiles_of(joined), w_reduce2, keep(narrowed_even, narrowed_odd, b_reduce2), 1, None),
            (tap(narrowed_even, narrowed_odd), w_spatial2, plain(spatial, b_spatial2), 1, turn_next),
            (tiles_of(spatial), w_expand2, pool, 1, None),
        ]
        accumulators = [
            pltpu.ACC(mxu)((LINE, mid), f32) for mxu in range(2) for _ in range(half)
        ]

        def whole(*accs):
            run(stages, *accs)
            rows = pl.ds(pl.multiple_of(batch * BATCH, BATCH), BATCH)
            for n, total in totals.items():
                pooled[rows, lanes(n)] = total / CELLS

        pl.run_scoped(whole, *accumulators)
        return 0

    lax.fori_loop(0, batches, encode, 0)

    rows = out.shape[0]
    width = pooled.shape[1] // mid
    cap = rows // (8 * width)
    row = lax.broadcasted_iota(jnp.int32, (rows, mid), 0)
    place = lax.broadcasted_iota(jnp.int32, (rows, mid), 1)
    column = lax.broadcasted_iota(jnp.int32, (rows, 1), 0)
    divisor = jnp.ones((rows, 1), f32)
    owners = [owner_ref[0, j] for j in range(slides)]
    chosen = jnp.zeros((rows, mid), f32)
    slot = row // (width * cap) * cap + row % cap
    slot_column = column // (width * cap) * cap + column % cap
    for j in range(slides):
        standing = jnp.int32(0)
        for earlier in range(j):
            standing += (owners[earlier] == owners[j]).astype(jnp.int32)
        target = owners[j] * cap + standing
        member = (slot == target) & (place >= ends[j] - counts[j]) & (place < ends[j])
        chosen = jnp.where(member, 1.0, chosen)
        size = jnp.maximum(counts[j], 1).astype(f32)
        divisor = jnp.where(slot_column == target, size, divisor)

    def average(acc):
        for n in range(width):
            pltpu.matmul_push_rhs(
                pooled[:, lanes(n)].astype(bf16), staging_register=n % 2, mxu_index=0
            )
            here = jnp.where(row // cap % width == n, chosen, 0.0).astype(bf16)
            pltpu.matmul_acc_lhs(acc, here, load_staged_rhs=n % 2)
        out[...] = (pltpu.matmul_pop(acc) / divisor).astype(bf16)

    pl.run_scoped(average, pltpu.ACC(0)((rows, mid), f32))


def deliver_kernel(packed, out, received, send_sem, receive_sem):
    bf16, f32 = jnp.bfloat16, jnp.float32
    loaders = lax.axis_size("loader")
    me = lax.axis_index("loader")
    size = packed.shape[0] // loaders

    def block(index):
        return pl.ds(pl.multiple_of(index * size, size), size)

    barrier = pltpu.get_barrier_semaphore()
    peers = [lax.rem(me + step, loaders) for step in range(1, loaders)]
    for peer in peers:
        pl.semaphore_signal(barrier, inc=1, device_id={"loader": peer}, device_id_type=MESH)
    pl.semaphore_wait(barrier, loaders - 1)
    copies = [
        pltpu.make_async_remote_copy(
            src_ref=packed.at[block(peer)],
            dst_ref=received.at[block(me)],
            send_sem=send_sem.at[index],
            recv_sem=receive_sem.at[index],
            device_id={"loader": peer},
            device_id_type=MESH,
        )
        for index, peer in enumerate(peers)
    ]
    for copy in copies:
        copy.start()
    received[block(me), :] = packed[block(me), :]
    for copy in copies:
        copy.wait()

    rows, lanes = out.shape[0], packed.shape[1]
    width = out.shape[1] // lanes
    cap = rows // loaders
    shape = (rows, packed.shape[0])
    row = lax.broadcasted_iota(jnp.int32, shape, 0)
    column = lax.broadcasted_iota(jnp.int32, shape, 1)
    for n in range(width):
        source = (row // cap * width + n) * cap + row % cap
        chosen = (column == source).astype(f32).astype(bf16)
        value = jnp.dot(chosen, received[...], preferred_element_type=f32)
        out[:, n * lanes : (n + 1) * lanes] = value.astype(bf16)


def encode_local(
    tiles,
    slide_counts,
    slide_owner,
    w_reduce,
    b_reduce,
    w_spatial,
    b_spatial,
    w_expand,
    w_short,
    b_join,
    w_reduce2,
    b_reduce2,
    w_spatial2,
    b_spatial2,
    w_expand2,
    b_expand2,
    loaders,
):
    bf16, f32 = jnp.bfloat16, jnp.float32
    places = tiles.shape[0] // CELLS
    c_in, c_mid = w_reduce.shape
    c_out = w_expand.shape[1]
    cap = places // loaders
    batches = places // BATCH
    smem = pl.BlockSpec(memory_space=pltpu.SMEM)
    vmem = pl.BlockSpec(memory_space=pltpu.VMEM)
    anywhere = pl.BlockSpec(memory_space=pl.ANY)
    bordered = (GRID + 2, PAIRS, 2 * BATCH, c_mid)
    return pl.pallas_call(
        encoder_kernel,
        out_shape=jax.ShapeDtypeStruct((loaders * (c_out // c_mid) * cap, c_mid), bf16),
        in_specs=[smem] * 2 + [vmem] * 6 + [anywhere] * 8,
        out_specs=vmem,
        scratch_shapes=[
            pltpu.VMEM(w_reduce.shape, bf16),
            pltpu.VMEM(w_spatial.shape, bf16),
            pltpu.VMEM((c_mid + c_in, c_out), bf16),
            pltpu.VMEM(w_reduce2.shape, bf16),
            pltpu.VMEM(w_spatial2.shape, bf16),
            pltpu.VMEM(w_expand2.shape, bf16),
            pltpu.VMEM((batches, ROWS, c_in), bf16),
            pltpu.VMEM((4, ROWS, 128), f32),
            pltpu.VMEM((ROWS, c_in), bf16),
            pltpu.VMEM(bordered, bf16),
            pltpu.VMEM(bordered, bf16),
            pltpu.VMEM(bordered, bf16),
            pltpu.VMEM(bordered, bf16),
            pltpu.VMEM((ROWS, c_mid), bf16),
            pltpu.VMEM((ROWS, c_out), bf16),
            pltpu.VMEM((ROWS, c_out), f32),
            pltpu.VMEM((c_mid, c_out), f32),
            pltpu.SemaphoreType.DMA((7,)),
            pltpu.SemaphoreType.DMA((batches,)),
        ],
        compiler_params=pltpu.CompilerParams(vmem_limit_bytes=60 * 1024 * 1024),
        name="encode_tiles",
    )(
        slide_counts,
        slide_owner.T,
        b_reduce[None],
        b_spatial[None],
        b_join[None],
        b_reduce2[None],
        b_spatial2[None],
        b_expand2[None],
        tiles,
        w_reduce,
        w_spatial,
        w_expand,
        w_short,
        w_reduce2,
        w_spatial2,
        w_expand2,
    )


def deliver(packed, places, c_out):
    vmem = pl.BlockSpec(memory_space=pltpu.VMEM)
    others = lax.axis_size("loader") - 1
    return pl.pallas_call(
        deliver_kernel,
        out_shape=jax.ShapeDtypeStruct((places, c_out), packed.dtype),
        in_specs=[vmem],
        out_specs=vmem,
        scratch_shapes=[
            pltpu.VMEM(packed.shape, packed.dtype),
            pltpu.SemaphoreType.DMA((others,)),
            pltpu.SemaphoreType.DMA((others,)),
        ],
        compiler_params=pltpu.CompilerParams(collective_id=0, has_side_effects=True),
        name="deliver_slides",
    )(packed)


def body(tiles, tile_encoder, tile_slot, slide_counts, slide_owner, *weights):
    packed = encode_local(
        tiles, slide_counts, slide_owner, *weights, loaders=lax.axis_size("loader")
    )
    return deliver(packed, tile_encoder.shape[0], weights[4].shape[1])


def solution(mesh):
    split = P(("loader", "enc"))
    placed = (split,) * 5 + (P(),) * 13
    return jax.shard_map(
        body, mesh=mesh, in_specs=placed, out_specs=split, check_vma=False
    )
```

time: 85.6 us -> 54.2 us (0.63)
  Pallas kernels: 69.7 us -> 52.5 us
  blocking collectives: 11.5 us -> 0 us
  local copies, waits for them, and re-layouts: 2.84 us -> 1.47 us
  other arithmetic: 1.33 us -> 0 us
    pallas_call x1 -> x2, Pallas kernels: 69.7 us -> 52.5 us  [the longest x1 33.6 us: encode_local(): pl.pallas_call(encoder_kernel, out_shape=jax.ShapeDtypeStruct((loaders *...]
    all_to_all x1 -> x0, blocking collectives: 11.5 us -> none  [body(): lax.all_to_all(packed.reshape(loaders, places // loaders, -1), 'loader',...]
    reshape x2 -> x0, local copies, waits for them, and re-layouts: 1.52 us -> none  [the longest x1 0.87 us: body(): packed.reshape(loaders, places // loaders, -1)]
    another operation x1 -> x0, other arithmetic: 1.33 us -> none  [body(): slide_end = jnp.cumsum(slide_counts, axis=1)]
where the time goes in v2:
time: 54.2 us; the launch traced here: 54 us
  Pallas kernels  52.5 us (97%)
  local copies, waits for them, and re-layouts  1.47 us (3%)
    pallas_call x1, Pallas kernels, encode_local(): pl.pallas_call(encoder_kernel, out_shape=jax.ShapeDtypeStruct((loaders *...  33.6 us
    pallas_call x1, Pallas kernels, deliver(): pl.pallas_call(deliver_kernel, out_shape=jax.ShapeDtypeStruct((places, c_...  18.9 us
    unnamed x1, local copies, waits for them, and re-layouts  1.47 us

profile of v2, /device:TPU:1, one launch (start us, length us, event | category | flops | bytes accessed | tf_op | source)
XLA Modules:
  0.0 54.0 jit_solution(11119861224181045249)
XLA Ops:
  0.0 33.6 %encode_tiles.1.packed = bf16[128,256]{1,0:T(8,128)(2,1)} custom-call(s32[1,8]{1,0:T(1,128)} %counts_ref.1, s32[1,8]{1,0:T(1,128)} %bitcast.13, f32[1,256]{1,0:T(1,128)} %bitcast.9, f32[1,256]{1,0:T(1,128)} %bitcast.10, f32[1,1024]{1,0:T(1,128)} %bitcast.7, f32[1,256]{1,0:T(1,128)} %bitcast.11, f32[1,256]{1,0:T(1,128)} %bitcast.12, f32[1,1024]{1,0:T(1,128)} %bitcast.8, ...), custom_call_target="tpu_custom_call" | custom-call | tf_op jit(solution)/shard_map/encode_tiles/pallas_call | solution.py:367
  33.6 18.9 %deliver_slides.1 = bf16[32,1024]{1,0:T(8,128)(2,1)} custom-call(bf16[128,256]{1,0:T(8,128)(2,1)} %encode_tiles.1.packed), custom_call_target="tpu_custom_call" | custom-call | tf_op jit(solution)/shard_map/deliver_slides/pallas_call | solution.py:418
  52.5 1.5 %copy.18 = bf16[32,1024]{1,0:T(8,128)(2,1)} copy(bf16[32,1024]{1,0:T(8,128)(2,1)} %deliver_slides.1) | data formatting | bytes 131072

commit v3 on v2

--- a/solution.py
+++ b/solution.py
@@ -51,8 +51,12 @@
     joined,
     residual,
     pooled,
+    packed,
+    received,
     weight_sem,
     tile_sem,
+    send_sem,
+    receive_sem,
 ):
     f32, bf16 = jnp.float32, jnp.bfloat16
     slides = counts_ref.shape[1]
@@ -62,7 +66,13 @@
     ends = [counts[0]]
     for count in counts[1:]:
         ends.append(ends[-1] + count)
-    batches = (ends[-1] + BATCH - 1) // BATCH
+
+    loaders = lax.axis_size("loader")
+    me = lax.axis_index("loader")
+    peers = [lax.rem(me + step, loaders) for step in range(1, loaders)]
+    barrier = pltpu.get_barrier_semaphore()
+    for peer in peers:
+        pl.semaphore_signal(barrier, inc=1, device_id={"loader": peer}, device_id_type=MESH)
 
     def tile_copy(batch):
         rows = pl.ds(pl.multiple_of(batch * ROWS, ROWS), ROWS)
@@ -81,17 +91,18 @@
         pltpu.make_async_copy(source, target, weight_sem.at[index])
         for index, (source, target) in enumerate(moves)
     ]
-    pl.when(batches > 0)(lambda: tile_copy(0).start())
+    tile_copy(0).start()
     for copy in copies:
         copy.start()
     for batch in range(1, most):
-        pl.when(batches > batch)(functools.partial(lambda b: tile_copy(b).start(), batch))
+        tile_copy(batch).start()
 
     border = jnp.zeros((1,) + reduced_even.shape[1:], bf16)
     for padded in (reduced_even, reduced_odd, narrowed_even, narrowed_odd):
         padded[0:1] = border
         padded[GRID + 1 : GRID + 2] = border
     pooled[...] = jnp.zeros_like(pooled)
+    received[packed.shape[0] :, :] = jnp.zeros((mid - packed.shape[0], mid), bf16)
 
     half = GRID // 2
     order = [(lane, k) for k in range(half) for lane in range(2)]
@@ -199,20 +210,18 @@
                 pair * 2 * BATCH : (pair + 1) * 2 * BATCH, lane * 128 : (lane + 1) * 128
             ] = jnp.concatenate(two, axis=0).astype(bf16)
 
-    @pl.when(batches > 0)
-    def _():
-        tile_copy(0).wait()
-        for i in range(GRID):
-            widen(0, i)
-        for pair in range(CELLS // 2):
-            turn(pair)
+    tile_copy(0).wait()
+    for i in range(GRID):
+        widen(0, i)
+    for pair in range(CELLS // 2):
+        turn(pair)
 
     for copy in copies:
         copy.wait()
 
     def encode(batch, _):
-        pl.when(batch + 1 < batches)(lambda: tile_copy(batch + 1).wait())
-        following = jnp.minimum(batch + 1, most - 1)
+        pl.when(batch + 1 < most)(lambda: tile_copy(batch + 1).wait())
+        following = lax.rem(batch + 1, most)
         totals = {}
 
         def widen_next(step):
@@ -256,11 +265,11 @@
         pl.run_scoped(whole, *accumulators)
         return 0
 
-    lax.fori_loop(0, batches, encode, 0)
-
-    rows = out.shape[0]
+    lax.fori_loop(0, most, encode, 0)
+
+    rows = packed.shape[0]
     width = pooled.shape[1] // mid
-    cap = rows // (8 * width)
+    cap = rows // (loaders * width)
     row = lax.broadcasted_iota(jnp.int32, (rows, mid), 0)
     place = lax.broadcasted_iota(jnp.int32, (rows, mid), 1)
     column = lax.broadcasted_iota(jnp.int32, (rows, 1), 0)
@@ -286,26 +295,17 @@
             )
             here = jnp.where(row // cap % width == n, chosen, 0.0).astype(bf16)
             pltpu.matmul_acc_lhs(acc, here, load_staged_rhs=n % 2)
-        out[...] = (pltpu.matmul_pop(acc) / divisor).astype(bf16)
+        packed[...] = (pltpu.matmul_pop(acc) / divisor).astype(bf16)
 
     pl.run_scoped(average, pltpu.ACC(0)((rows, mid), f32))
 
-
-def deliver_kernel(packed, out, received, send_sem, receive_sem):
-    bf16, f32 = jnp.bfloat16, jnp.float32
-    loaders = lax.axis_size("loader")
-    me = lax.axis_index("loader")
-    size = packed.shape[0] // loaders
+    size = width * cap
 
     def block(index):
         return pl.ds(pl.multiple_of(index * size, size), size)
 
-    barrier = pltpu.get_barrier_semaphore()
-    peers = [lax.rem(me + step, loaders) for step in range(1, loaders)]
-    for peer in peers:
-        pl.semaphore_signal(barrier, inc=1, device_id={"loader": peer}, device_id_type=MESH)
     pl.semaphore_wait(barrier, loaders - 1)
-    copies = [
+    sends = [
         pltpu.make_async_remote_copy(
             src_ref=packed.at[block(peer)],
             dst_ref=received.at[block(me)],
@@ -316,23 +316,26 @@
         )
         for index, peer in enumerate(peers)
     ]
-    for copy in copies:
-        copy.start()
+    for send in sends:
+        send.start()
     received[block(me), :] = packed[block(me), :]
-    for copy in copies:
-        copy.wait()
-
-    rows, lanes = out.shape[0], packed.shape[1]
-    width = out.shape[1] // lanes
-    cap = rows // loaders
-    shape = (rows, packed.shape[0])
+
+    shape = (out.shape[0], mid)
     row = lax.broadcasted_iota(jnp.int32, shape, 0)
     column = lax.broadcasted_iota(jnp.int32, shape, 1)
-    for n in range(width):
-        source = (row // cap * width + n) * cap + row % cap
-        chosen = (column == source).astype(f32).astype(bf16)
-        value = jnp.dot(chosen, received[...], preferred_element_type=f32)
-        out[:, n * lanes : (n + 1) * lanes] = value.astype(bf16)
+
+    def unpack(*accs):
+        pltpu.matmul_push_rhs(received[...], staging_register=0, mxu_index=0)
+        for n, acc in enumerate(accs):
+            source = (row // cap * width + n) * cap + row % cap
+            here = jnp.where(column == source, 1.0, 0.0).astype(bf16)
+            pltpu.matmul_acc_lhs(acc, here, load_staged_rhs=0 if n == 0 else None)
+        for n, acc in enumerate(accs):
+            out[:, lanes(n)] = pltpu.matmul_pop(acc).astype(bf16)
+
+    for send in sends:
+        send.wait()
+    pl.run_scoped(unpack, *[pltpu.ACC(0)(shape, f32) for _ in range(width)])
 
 
 def encode_local(
@@ -352,13 +355,13 @@
     b_spatial2,
     w_expand2,
     b_expand2,
-    loaders,
 ):
     bf16, f32 = jnp.bfloat16, jnp.float32
     places = tiles.shape[0] // CELLS
     c_in, c_mid = w_reduce.shape
     c_out = w_expand.shape[1]
-    cap = places // loaders
+    loaders = lax.axis_size("loader")
+    packed_rows = places * (c_out // c_mid)
     batches = places // BATCH
     smem = pl.BlockSpec(memory_space=pltpu.SMEM)
     vmem = pl.BlockSpec(memory_space=pltpu.VMEM)
@@ -366,7 +369,7 @@
     bordered = (GRID + 2, PAIRS, 2 * BATCH, c_mid)
     return pl.pallas_call(
         encoder_kernel,
-        out_shape=jax.ShapeDtypeStruct((loaders * (c_out // c_mid) * cap, c_mid), bf16),
+        out_shape=jax.ShapeDtypeStruct((places, c_out), bf16),
         in_specs=[smem] * 2 + [vmem] * 6 + [anywhere] * 8,
         out_specs=vmem,
         scratch_shapes=[
@@ -387,10 +390,16 @@
             pltpu.VMEM((ROWS, c_out), bf16),
             pltpu.VMEM((ROWS, c_out), f32),
             pltpu.VMEM((c_mid, c_out), f32),
+            pltpu.VMEM((packed_rows, c_mid), bf16),
+            pltpu.VMEM((c_mid, c_mid), bf16),
             pltpu.SemaphoreType.DMA((7,)),
             pltpu.SemaphoreType.DMA((batches,)),
+            pltpu.SemaphoreType.DMA((loaders - 1,)),
+            pltpu.SemaphoreType.DMA((loaders - 1,)),
         ],
-        compiler_params=pltpu.CompilerParams(vmem_limit_bytes=60 * 1024 * 1024),
+        compiler_params=pltpu.CompilerParams(
+            vmem_limit_bytes=60 * 1024 * 1024, collective_id=0, has_side_effects=True
+        ),
         name="encode_tiles",
     )(
         slide_counts,
@@ -412,29 +421,8 @@
     )
 
 
-def deliver(packed, places, c_out):
-    vmem = pl.BlockSpec(memory_space=pltpu.VMEM)
-    others = lax.axis_size("loader") - 1
-    return pl.pallas_call(
-        deliver_kernel,
-        out_shape=jax.ShapeDtypeStruct((places, c_out), packed.dtype),
-        in_specs=[vmem],
-        out_specs=vmem,
-        scratch_shapes=[
-            pltpu.VMEM(packed.shape, packed.dtype),
-            pltpu.SemaphoreType.DMA((others,)),
-            pltpu.SemaphoreType.DMA((others,)),
-        ],
-        compiler_params=pltpu.CompilerParams(collective_id=0, has_side_effects=True),
-        name="deliver_slides",
-    )(packed)
-
-
 def body(tiles, tile_encoder, tile_slot, slide_counts, slide_owner, *weights):
-    packed = encode_local(
-        tiles, slide_counts, slide_owner, *weights, loaders=lax.axis_size("loader")
-    )
-    return deliver(packed, tile_encoder.shape[0], weights[4].shape[1])
+    return encode_local(tiles, slide_counts, slide_owner, *weights)
 
 
 def solution(mesh):

time: 54.2 us -> 51.8 us (0.956)
  Pallas kernels: 52.5 us -> 50.1 us
    pallas_call x2 -> x1, Pallas kernels: 52.5 us -> 50.1 us  [encode_local(): pl.pallas_call(encoder_kernel, out_shape=jax.ShapeDtypeStruct((places, c_...]
where the time goes in v3:
time: 51.8 us; the launch traced here: 51.6 us
  Pallas kernels  50.1 us (97%)
  local copies, waits for them, and re-layouts  1.47 us (3%)
    pallas_call x1, Pallas kernels, encode_local(): pl.pallas_call(encoder_kernel, out_shape=jax.ShapeDtypeStruct((places, c_...  50.1 us
    unnamed x1, local copies, waits for them, and re-layouts  1.47 us

profile of v3, /device:TPU:1, one launch (start us, length us, event | category | flops | bytes accessed | tf_op | source)
XLA Modules:
  0.0 51.6 jit_solution(6102972194811572762)
XLA Ops:
  0.0 50.1 %encode_tiles.1 = bf16[32,1024]{1,0:T(8,128)(2,1)} custom-call(s32[1,8]{1,0:T(1,128)} %counts_ref.1, s32[1,8]{1,0:T(1,128)} %bitcast.13, f32[1,256]{1,0:T(1,128)} %bitcast.9, f32[1,256]{1,0:T(1,128)} %bitcast.10, f32[1,1024]{1,0:T(1,128)} %bitcast.7, f32[1,256]{1,0:T(1,128)} %bitcast.11, f32[1,256]{1,0:T(1,128)} %bitcast.12, f32[1,1024]{1,0:T(1,128)} %bitcast.8, ...), custom_call_target="tpu_custom_call" | custom-call | tf_op jit(solution)/shard_map/encode_tiles/pallas_call | solution.py:370
  50.1 1.5 %copy.18 = bf16[32,1024]{1,0:T(8,128)(2,1)} copy(bf16[32,1024]{1,0:T(8,128)(2,1)} %encode_tiles.1) | data formatting | bytes 131072

commit v4 on v3

--- a/solution.py
+++ b/solution.py
@@ -43,10 +43,13 @@
     arrived,
     widened,
     pixels,
-    reduced_even,
-    reduced_odd,
-    narrowed_even,
-    narrowed_odd,
+    w_mixed,
+    w_mixed2,
+    even,
+    odd,
+    plane,
+    sums,
+    differences,
     spatial,
     joined,
     residual,
@@ -79,12 +82,12 @@
         return pltpu.make_async_copy(tiles.at[rows], arrived.at[batch], tile_sem.at[batch])
 
     moves = [
+        (w_spatial_hbm, w_spatial),
+        (w_spatial2_hbm, w_spatial2),
         (w_reduce_hbm, w_reduce),
-        (w_spatial_hbm, w_spatial),
         (w_expand_hbm, w_join.at[pl.ds(0, mid)]),
         (w_short_hbm, w_join.at[pl.ds(mid, w_short_hbm.shape[0])]),
         (w_reduce2_hbm, w_reduce2),
-        (w_spatial2_hbm, w_spatial2),
         (w_expand2_hbm, w_expand2),
     ]
     copies = [
@@ -97,81 +100,127 @@
     for batch in range(1, most):
         tile_copy(batch).start()
 
-    border = jnp.zeros((1,) + reduced_even.shape[1:], bf16)
-    for padded in (reduced_even, reduced_odd, narrowed_even, narrowed_odd):
-        padded[0:1] = border
-        padded[GRID + 1 : GRID + 2] = border
     pooled[...] = jnp.zeros_like(pooled)
     received[packed.shape[0] :, :] = jnp.zeros((mid - packed.shape[0], mid), bf16)
 
     half = GRID // 2
-    order = [(lane, k) for k in range(half) for lane in range(2)]
-
-    def image_row(mxu, k):
-        return k if mxu == 0 else GRID - 1 - k
-
-    def keep(even, odd, bias):
-        def finish(i, n, value):
-            value = jnp.maximum(value + bias[...], 0.0).reshape(GRID, BATCH, mid)
-            side = jnp.zeros((1, BATCH, mid), f32)
-            whole = jnp.concatenate([side, value, side], axis=0)
-            even[i + 1] = whole.reshape(PAIRS, 2 * BATCH, mid).astype(bf16)
-            odd[i + 1, 0 : PAIRS - 1] = value.reshape(
-                PAIRS - 1, 2 * BATCH, mid
-            ).astype(bf16)
-
-        return finish
-
-    def tap(even, odd):
-        def left(i, k):
-            a, b = k // 3, k % 3
-            source = odd if b == 1 else even
-            first = 1 if b == 2 else 0
-            piece = source[i + a, first : first + PAIRS - 1]
-            return piece.reshape(LINE, mid)
-
-        return left
-
-    def line(i):
-        return slice(i * LINE, (i + 1) * LINE)
+    pieces = PAIRS - 1
+    pair = 2 * BATCH
+
+    def at(i, j):
+        return i * pieces + j
 
     def lanes(n):
         return slice(n * mid, (n + 1) * mid)
 
-    def plain(target, bias):
-        def finish(i, n, value):
-            value = jnp.maximum(value + bias[:, lanes(n)], 0.0).astype(bf16)
-            target[line(i), lanes(n)] = value
+    held = {}
+
+    def spread_row(q, m, j, value):
+        odd[q, m, j] = value.astype(bf16)
+        before = held[q] if j else jnp.zeros((BATCH, mid), f32)
+        even[q, m, j] = jnp.concatenate([before, value[:BATCH]], axis=0).astype(bf16)
+        held[q] = value[BATCH:]
+        if j == pieces - 1:
+            after = jnp.zeros((BATCH, mid), f32)
+            even[q, m, j + 1] = jnp.concatenate([held[q], after], axis=0).astype(bf16)
+
+    def keep(bias):
+        def finish(m, j, n, first, second):
+            first = jnp.maximum(first + bias[...], 0.0)
+            second = jnp.maximum(second + bias[...], 0.0)
+            plane[at(2 * m, j)] = first
+            plane[at(2 * m + 1, j)] = second
+            spread_row(1, m, j, first + second)
+            spread_row(2, m, j, second - first)
 
         return finish
 
-    def join(i, n, value):
-        value = jnp.maximum(value + b_join[:, lanes(n)], 0.0)
-        joined[line(i), lanes(n)] = value.astype(bf16)
-        residual[line(i), lanes(n)] = value + b_expand2[:, lanes(n)]
-
-    def tiles_of(ref):
-        return lambda i, k: ref[line(i), lanes(k)]
+    def outer(m, nothing):
+        for j in range(pieces):
+            rows = {
+                i: plane[at(i, j) + nothing] for i in range(2 * m - 1, 2 * m + 3) if 0 <= i < GRID
+            }
+            low = -rows[2 * m + 1]
+            if 2 * m - 1 in rows:
+                low = rows[2 * m - 1] + low
+            high = rows[2 * m]
+            if 2 * m + 2 in rows:
+                high = high - rows[2 * m + 2]
+            spread_row(0, m, j, low)
+            spread_row(3, m, j, high)
+
+    combination = ((1, 0), (2, 3))
+
+    def tap(mxu, m, j, n, k):
+        q = combination[mxu][n]
+        return odd[q, m, j] if k == 1 else even[q, m, j + k // 2]
+
+    def taps(plain, mixed):
+        def weights(mxu, n, k):
+            q = combination[mxu][n]
+            if q in (1, 2):
+                return mixed[q - 1, k]
+            return plain[lanes((6 if q == 3 else 0) + k)]
+
+        return weights
+
+    def mix(plain, mixed):
+        for k in range(3):
+            for part in range(4):
+                rows = [
+                    plain[(3 * a + k) * mid + part * 64 : (3 * a + k) * mid + part * 64 + 64]
+                    for a in range(3)
+                ]
+                rows = [row.astype(f32) * 0.5 for row in rows]
+                ends = rows[0] + rows[2]
+                mixed[0, k, part * 64 : part * 64 + 64] = (ends + rows[1]).astype(bf16)
+                mixed[1, k, part * 64 : part * 64 + 64] = (ends - rows[1]).astype(bf16)
+
+    def convolved(bias, nothing):
+        def finish(m, j, n, first, second):
+            if n == 0:
+                sums[at(m, j)] = first + second
+                differences[at(m, j)] = first - second
+                return
+            first = first + sums[at(m, j) + nothing] + bias[...]
+            second = differences[at(m, j) + nothing] - second + bias[...]
+            spatial[at(2 * m, j)] = jnp.maximum(first, 0.0).astype(bf16)
+            spatial[at(2 * m + 1, j)] = jnp.maximum(second, 0.0).astype(bf16)
+
+        return finish
+
+    def join(m, j, n, *values):
+        for i, value in enumerate(values, 2 * m):
+            value = jnp.maximum(value + b_join[:, lanes(n)], 0.0)
+            joined[at(i, j), :, lanes(n)] = value.astype(bf16)
+            residual[at(i, j), :, lanes(n)] = value + b_expand2[:, lanes(n)]
+
+    def tiles_of(ref, nothing):
+        return lambda mxu, m, j, n, k: ref[at(2 * m + mxu, j) + nothing, :, lanes(k)]
+
+    def whole(ref):
+        return lambda mxu, n, k: ref[lanes(k), lanes(n)]
 
     def run(stages, *accs):
         passes = []
-        for left, weights, finish, lag, beside in stages:
-            depth, width = weights.shape[0] // mid, weights.shape[1] // mid
+        for left, weights, width, depth, finish, lag, beside in stages:
             for n in range(width):
                 for k in range(depth):
-                    ahead = lag if n == 0 else 0
+                    ahead = lag if n == 0 else None
                     passes.append((left, weights, finish, n, k, k == depth - 1, ahead, beside))
 
         def push(index):
             _, weights, _, n, k, _, _, _ = passes[index]
             for mxu in range(2):
                 pltpu.matmul_push_rhs(
-                    weights[lanes(k), lanes(n)], staging_register=index % 2, mxu_index=mxu
+                    weights(mxu, n, k), staging_register=index % 2, mxu_index=mxu
                 )
 
-        def pop(finish, n, k):
-            for mxu in range(2):
-                finish(image_row(mxu, k), n, pltpu.matmul_pop(accs[mxu * half + k]))
+        def acc(mxu, block, j):
+            return accs[(mxu * half + block) * pieces + j]
+
+        def pop(finish, n, block, j):
+            finish(block, j, n, *[pltpu.matmul_pop(acc(mxu, block, j)) for mxu in range(2)])
 
         push(0)
         waiting = None
@@ -180,89 +229,110 @@
                 push(index + 1)
             popped = 0
             for block in range(half):
+                if waiting is not None and lag is not None:
+                    while popped < min(half, block + 1 + lag):
+                        for j in range(pieces):
+                            pop(*waiting, popped, j)
+                        popped += 1
                 if beside is not None:
-                    beside(k * half + block)
-                if waiting is not None:
-                    while popped < min(half, block + 1 + lag):
-                        pop(*waiting, popped)
-                        popped += 1
-                for mxu in range(2):
-                    pltpu.matmul_acc_lhs(
-                        accs[mxu * half + block],
-                        left(image_row(mxu, block), k),
-                        load_staged_rhs=index % 2 if block == 0 else None,
-                    )
+                    beside(n, k, block)
+                for j in range(pieces):
+                    if waiting is not None and lag is None:
+                        pop(*waiting, block, j)
+                    for mxu in range(2):
+                        pltpu.matmul_acc_lhs(
+                            acc(mxu, block, j),
+                            left(mxu, block, j, n, k),
+                            load_staged_rhs=index % 2 if block + j == 0 else None,
+                        )
             waiting = (finish, n) if last else None
         for block in range(half):
-            pop(*waiting, block)
+            for j in range(pieces):
+                pop(*waiting, block, j)
 
     def widen(batch, i):
-        block = arrived[batch, line(i), :].astype(f32)
+        line = slice(i * LINE, (i + 1) * LINE)
+        block = arrived[batch, line, :].astype(f32)
         for lane in range(4):
-            widened[lane, line(i), :] = block[:, lane * 128 : (lane + 1) * 128]
-
-    def turn(pair):
+            widened[lane, line, :] = block[:, lane * 128 : (lane + 1) * 128]
+
+    def turn(two_places):
         for lane in range(4):
             two = [
-                widened[lane, pl.ds(2 * pair + k, BATCH, stride=CELLS), :] for k in range(2)
+                widened[lane, pl.ds(2 * two_places + k, BATCH, stride=CELLS), :] for k in range(2)
             ]
-            pixels[
-                pair * 2 * BATCH : (pair + 1) * 2 * BATCH, lane * 128 : (lane + 1) * 128
-            ] = jnp.concatenate(two, axis=0).astype(bf16)
+            pixels[two_places, :, lane * 128 : (lane + 1) * 128] = jnp.concatenate(two, axis=0).astype(bf16)
 
     tile_copy(0).wait()
     for i in range(GRID):
         widen(0, i)
-    for pair in range(CELLS // 2):
-        turn(pair)
-
-    for copy in copies:
+    for two_places in range(CELLS // 2):
+        turn(two_places)
+
+    copies[0].wait()
+    mix(w_spatial, w_mixed)
+    copies[1].wait()
+    mix(w_spatial2, w_mixed2)
+    for copy in copies[2:]:
         copy.wait()
 
     def encode(batch, _):
         pl.when(batch + 1 < most)(lambda: tile_copy(batch + 1).wait())
         following = lax.rem(batch + 1, most)
         totals = {}
-
-        def widen_next(step):
-            if step % 4 == 0 and step // 4 < GRID:
-                widen(following, step // 4)
-
-        def turn_next(step):
-            for pair in (2 * step, 2 * step + 1):
-                if pair < CELLS // 2:
-                    turn(pair)
-
-        def pool(i, n, value):
-            value = jnp.maximum(value + residual[line(i), lanes(n)], 0.0)
-            value = value.reshape(GRID, BATCH, mid)
-            value = jnp.sum(value, axis=0)
-            totals[n] = totals[n] + value if n in totals else value
-
-        def both(i, k):
+        nothing = lax.rem(batch * (batch + 1), 2)
+
+        def first_side(n, k, block):
+            if n == 0 and k > 0 and block % 2 == 0 and (k - 1) * 4 + block // 2 < half:
+                outer((k - 1) * 4 + block // 2, nothing)
+            if n == 1:
+                step = k * half + block
+                if step < GRID:
+                    widen(following, step)
+
+        def second_side(n, k, block):
+            if n == 0 and k > 0 and block % 2 == 0 and (k - 1) * 4 + block // 2 < half:
+                outer((k - 1) * 4 + block // 2, nothing)
+            if n == 1:
+                step = k * half + block
+                for two_places in range(5 * step, 5 * step + 5):
+                    if two_places < CELLS // 2:
+                        turn(two_places)
+
+        def pool(m, j, n, *values):
+            for i, value in enumerate(values, 2 * m):
+                value = jnp.maximum(value + residual[at(i, j) + nothing, :, lanes(n)], 0.0)
+                value = value[:BATCH] + value[BATCH:]
+                totals[n] = totals[n] + value if n in totals else value
+
+        def both(mxu, m, j, n, k):
             if k == 0:
-                return spatial[line(i), :]
-            return pixels[line(i), lanes(k - 1)]
-
+                return spatial[at(2 * m + mxu, j) + nothing]
+            return pixels[at(2 * m + mxu, j), :, lanes(k - 1)]
+
+        wide = joined.shape[2] // mid
+        deep = pixels.shape[2] // mid
         stages = [
-            (tiles_of(pixels), w_reduce, keep(reduced_even, reduced_odd, b_reduce), 0, None),
-            (tap(reduced_even, reduced_odd), w_spatial, plain(spatial, b_spatial), 1, widen_next),
-            (both, w_join, join, 1, None),
-            (tiles_of(joined), w_reduce2, keep(narrowed_even, narrowed_odd, b_reduce2), 1, None),
-            (tap(narrowed_even, narrowed_odd), w_spatial2, plain(spatial, b_spatial2), 1, turn_next),
-            (tiles_of(spatial), w_expand2, pool, 1, None),
+            (tiles_of(pixels, 0), whole(w_reduce), 1, deep, keep(b_reduce), 0, None),
+            (tap, taps(w_spatial, w_mixed), 2, 3, convolved(b_spatial, nothing), 1, first_side),
+            (both, whole(w_join), wide, deep + 1, join, 1, None),
+            (tiles_of(joined, nothing), whole(w_reduce2), 1, wide, keep(b_reduce2), 1, None),
+            (tap, taps(w_spatial2, w_mixed2), 2, 3, convolved(b_spatial2, nothing), 1, second_side),
+            (tiles_of(spatial, nothing), whole(w_expand2), wide, 1, pool, 1, None),
         ]
         accumulators = [
-            pltpu.ACC(mxu)((LINE, mid), f32) for mxu in range(2) for _ in range(half)
+            pltpu.ACC(mxu)((pair, mid), f32)
+            for mxu in range(2)
+            for _ in range(half * pieces)
         ]
 
-        def whole(*accs):
+        def all_stages(*accs):
             run(stages, *accs)
             rows = pl.ds(pl.multiple_of(batch * BATCH, BATCH), BATCH)
             for n, total in totals.items():
                 pooled[rows, lanes(n)] = total / CELLS
 
-        pl.run_scoped(whole, *accumulators)
+        pl.run_scoped(all_stages, *accumulators)
         return 0
 
     lax.fori_loop(0, most, encode, 0)
@@ -366,7 +436,6 @@
     smem = pl.BlockSpec(memory_space=pltpu.SMEM)
     vmem = pl.BlockSpec(memory_space=pltpu.VMEM)
     anywhere = pl.BlockSpec(memory_space=pl.ANY)
-    bordered = (GRID + 2, PAIRS, 2 * BATCH, c_mid)
     return pl.pallas_call(
         encoder_kernel,
         out_shape=jax.ShapeDtypeStruct((places, c_out), bf16),
@@ -381,14 +450,17 @@
             pltpu.VMEM(w_expand2.shape, bf16),
             pltpu.VMEM((batches, ROWS, c_in), bf16),
             pltpu.VMEM((4, ROWS, 128), f32),
-            pltpu.VMEM((ROWS, c_in), bf16),
-            pltpu.VMEM(bordered, bf16),
-            pltpu.VMEM(bordered, bf16),
-            pltpu.VMEM(bordered, bf16),
-            pltpu.VMEM(bordered, bf16),
-            pltpu.VMEM((ROWS, c_mid), bf16),
-            pltpu.VMEM((ROWS, c_out), bf16),
-            pltpu.VMEM((ROWS, c_out), f32),
+            pltpu.VMEM((CELLS // 2, 2 * BATCH, c_in), bf16),
+            pltpu.VMEM((2, 3, c_mid, c_mid), bf16),
+            pltpu.VMEM((2, 3, c_mid, c_mid), bf16),
+            pltpu.VMEM((4, GRID // 2, PAIRS, 2 * BATCH, c_mid), bf16),
+            pltpu.VMEM((4, GRID // 2, PAIRS - 1, 2 * BATCH, c_mid), bf16),
+            pltpu.VMEM((CELLS // 2, 2 * BATCH, c_mid), f32),
+            pltpu.VMEM((CELLS // 4, 2 * BATCH, c_mid), f32),
+            pltpu.VMEM((CELLS // 4, 2 * BATCH, c_mid), f32),
+            pltpu.VMEM((CELLS // 2, 2 * BATCH, c_mid), bf16),
+            pltpu.VMEM((CELLS // 2, 2 * BATCH, c_out), bf16),
+            pltpu.VMEM((CELLS // 2, 2 * BATCH, c_out), f32),
             pltpu.VMEM((c_mid, c_out), f32),
             pltpu.VMEM((packed_rows, c_mid), bf16),
             pltpu.VMEM((c_mid, c_mid), bf16),

time: 51.8 us -> 47.7 us (0.921)
  Pallas kernels: 50.1 us -> 46.1 us
    pallas_call x1, Pallas kernels: 50.1 us -> 46.1 us  [encode_local(): pl.pallas_call(encoder_kernel, out_shape=jax.ShapeDtypeStruct((places, c_...]
where the time goes in v4:
time: 47.7 us; the launch traced here: 47.6 us
  Pallas kernels  46.1 us (97%)
  local copies, waits for them, and re-layouts  1.47 us (3%)
    pallas_call x1, Pallas kernels, encode_local(): pl.pallas_call(encoder_kernel, out_shape=jax.ShapeDtypeStruct((places, c_...  46.1 us
    unnamed x1, local copies, waits for them, and re-layouts  1.47 us

profile of v4, /device:TPU:1, one launch (start us, length us, event | category | flops | bytes accessed | tf_op | source)
XLA Modules:
  0.0 47.6 jit_solution(3614668346776839010)
XLA Ops:
  0.0 46.1 %encode_tiles.1 = bf16[32,1024]{1,0:T(8,128)(2,1)} custom-call(s32[1,8]{1,0:T(1,128)} %counts_ref.1, s32[1,8]{1,0:T(1,128)} %bitcast.13, f32[1,256]{1,0:T(1,128)} %bitcast.9, f32[1,256]{1,0:T(1,128)} %bitcast.10, f32[1,1024]{1,0:T(1,128)} %bitcast.7, f32[1,256]{1,0:T(1,128)} %bitcast.11, f32[1,256]{1,0:T(1,128)} %bitcast.12, f32[1,1024]{1,0:T(1,128)} %bitcast.8, ...), custom_call_target="tpu_custom_call" | custom-call | tf_op jit(solution)/shard_map/encode_tiles/pallas_call | solution.py:439
  46.1 1.5 %copy.18 = bf16[32,1024]{1,0:T(8,128)(2,1)} copy(bf16[32,1024]{1,0:T(8,128)(2,1)} %encode_tiles.1) | data formatting | bytes 131072

commit v5 on v4

--- a/solution.py
+++ b/solution.py
@@ -277,18 +277,18 @@
         copy.wait()
 
     def encode(batch, _):
-        pl.when(batch + 1 < most)(lambda: tile_copy(batch + 1).wait())
-        following = lax.rem(batch + 1, most)
+        @pl.when(batch + 1 < most)
+        def _():
+            tile_copy(batch + 1).wait()
+            for i in range(GRID):
+                widen(batch + 1, i)
+
         totals = {}
         nothing = lax.rem(batch * (batch + 1), 2)
 
         def first_side(n, k, block):
             if n == 0 and k > 0 and block % 2 == 0 and (k - 1) * 4 + block // 2 < half:
                 outer((k - 1) * 4 + block // 2, nothing)
-            if n == 1:
-                step = k * half + block
-                if step < GRID:
-                    widen(following, step)
 
         def second_side(n, k, block):
             if n == 0 and k > 0 and block % 2 == 0 and (k - 1) * 4 + block // 2 < half:

time: 47.7 us -> 47.2 us (0.990)
  Pallas kernels: 46.1 us -> 45.5 us
    pallas_call x1, Pallas kernels: 46.1 us -> 45.5 us  [encode_local(): pl.pallas_call(encoder_kernel, out_shape=jax.ShapeDtypeStruct((places, c_...]
where the time goes in v5:
time: 47.2 us; the launch traced here: 47 us
  Pallas kernels  45.5 us (96%)
  local copies, waits for them, and re-layouts  1.47 us (3%)
    pallas_call x1, Pallas kernels, encode_local(): pl.pallas_call(encoder_kernel, out_shape=jax.ShapeDtypeStruct((places, c_...  45.5 us
    unnamed x1, local copies, waits for them, and re-layouts  1.47 us

profile of v5, /device:TPU:1, one launch (start us, length us, event | category | flops | bytes accessed | tf_op | source)
XLA Modules:
  0.0 47.0 jit_solution(2607995199764293080)
XLA Ops:
  0.0 45.5 %encode_tiles.1 = bf16[32,1024]{1,0:T(8,128)(2,1)} custom-call(s32[1,8]{1,0:T(1,128)} %counts_ref.1, s32[1,8]{1,0:T(1,128)} %bitcast.13, f32[1,256]{1,0:T(1,128)} %bitcast.9, f32[1,256]{1,0:T(1,128)} %bitcast.10, f32[1,1024]{1,0:T(1,128)} %bitcast.7, f32[1,256]{1,0:T(1,128)} %bitcast.11, f32[1,256]{1,0:T(1,128)} %bitcast.12, f32[1,1024]{1,0:T(1,128)} %bitcast.8, ...), custom_call_target="tpu_custom_call" | custom-call | tf_op jit(solution)/shard_map/encode_tiles/pallas_call | solution.py:439
  45.6 1.5 %copy.18 = bf16[32,1024]{1,0:T(8,128)(2,1)} copy(bf16[32,1024]{1,0:T(8,128)(2,1)} %encode_tiles.1) | data formatting | bytes 131072
